TPU v7x, 32 devices: a whole 2x2x4 slice. The times are simulated.
32 devices in a mesh: seq: 8 (over y, x, core), tp: 4 (over z).
Axes of the slice: x: 2, y: 2, z: 4, core: 2. Of those that a mesh axis runs over, the one named last changes fastest.
Arguments:
- patches: bfloat16 [3072, 768], P(('seq', 'tp')), may hold values from -6 to 6
- specials: bfloat16 [20, 768], P('tp'), may hold values from -6 to 6
- pos_table: bfloat16 [1625, 768], replicated, may hold values from -3 to 3
- image_length: int32 [4], replicated, may hold values from 256 to 1369, as said below
- slot_band: int32 [48], replicated, may hold values from 0 to 47, as said below
- w_qkv: bfloat16 [3, 768, 768], P(None, None, 'tp'), may hold values from -0.21875 to 0.21875
- qv_bias: float32 [2, 768], P(None, 'tp'), may hold values from -2 to 2
- w_out: bfloat16 [768, 768], P('tp'), may hold values from -3 to 3
- branch_bias: float32 [2, 768], replicated, may hold values from -2 to 2
- ln_gain: float32 [2, 768], replicated, may hold values from 0.5 to 1.5
- ln_bias: float32 [2, 768], replicated, may hold values from -2 to 2
- layer_scale: float32 [2, 768], replicated, may hold values from 0.5 to 1.5
- w_up: bfloat16 [768, 3072], P(None, 'tp'), may hold values from -0.21875 to 0.21875
- up_bias: float32 [3072], P('tp'), may hold values from -2 to 2
- w_down: bfloat16 [3072, 768], P('tp'), may hold values from -0.109375 to 0.109375
- cot_patch: bfloat16 [3072, 768], P('seq'), may hold values from -6 to 6
- cot_special: bfloat16 [20, 768], replicated, may hold values from -6 to 6
Outputs:
- out_patch: bfloat16 [3072, 768], P(('seq', 'tp'))
- out_special: bfloat16 [20, 768], P('tp')
- grad_patch: float32 [3072, 768], P(('seq', 'tp'))
- grad_special: float32 [20, 768], P('tp')
- grad_pos: float32 [1625, 768], replicated
- grad_qkv: float32 [3, 768, 768], P(None, None, 'tp')
- grad_qv_bias: float32 [2, 768], P(None, 'tp')
- grad_out: float32 [768, 768], P('tp')
- grad_branch_bias: float32 [2, 768], replicated
- grad_ln_gain: float32 [2, 768], replicated
- grad_ln_bias: float32 [2, 768], replicated
- grad_layer_scale: float32 [2, 768], replicated
- grad_up: float32 [768, 3072], P(None, 'tp')
- grad_up_bias: float32 [3072], P('tp')
- grad_down: float32 [3072, 768], P('tp')
Inputs may be any that keep to these rules, and one draw needn't show every extreme that they name: `image_length`: exactly 1 of the 4 images have 1369 patches and the others 256. `slot_band`: a permutation of the band numbers; bands are numbered image by image from 0, each image taking ceil(length / 64) consecutive numbers, and numbers past the last image's bands are empty.
All inputs are finite; a program needn't handle non-finite values.
Results may differ from a plain program's by a relative error of at most 0.023.
Values may be sent and summed in bfloat16 or wider, within the bound.
No kernel may reach another device: no remote copies, remote signals or barrier semaphores. Data moves between devices by JAX's collectives and lax.ppermute only.
A program may use at most 128 MiB of HBM per device.

v0:
```python
import math

import jax
import jax.numpy as jnp
from jax import lax
from jax.sharding import PartitionSpec as P

DH = 64
SPECIALS = 5
PATCH_BIG = 1369
BAND = 64


eps_norm = 1e-06
masked_score = -1e30
key_block = 2048


def combined_all(value, axis, join):
    gathered = jax.tree.map(
        lambda a, kind: lax.all_gather(a.astype(kind), axis),
        value,
        jax.tree.map(lambda a: jnp.bfloat16 if a.dtype == jnp.float32 else a.dtype, value),
    )

    def take(source):
        return jax.tree.map(
            lambda a, own: lax.dynamic_index_in_dim(a, source, 0, False).astype(own.dtype),
            gathered,
            value,
        )

    return lax.fori_loop(
        1, lax.axis_size(axis), lambda source, state: join(state, take(source)), take(0)
    )


def shifted(value, axis, by):
    peers = lax.axis_size(axis)
    return lax.ppermute(value, axis, [(i, (i + by) % peers) for i in range(peers)])


def band_layout(image_length, slot_band):
    image_count = image_length.shape[0]
    band_counts = (image_length + BAND - 1) // BAND
    band_starts = jnp.cumsum(band_counts) - band_counts
    used_bands = jnp.sum(band_counts)
    passed = (slot_band[:, None] >= band_starts[None, :]).astype(jnp.int32)
    holder = jnp.sum(passed, axis=1) - 1
    picked = holder[:, None] == jnp.arange(image_count, dtype=jnp.int32)[None, :]
    first_band = jnp.sum(jnp.where(picked, band_starts[None, :], 0), axis=1)
    holder_length = jnp.sum(jnp.where(picked, image_length[None, :], 0), axis=1)
    within = (slot_band - first_band)[:, None] * BAND + jnp.arange(BAND, dtype=jnp.int32)[None, :]
    usable = (slot_band < used_bands)[:, None] & (within < holder_length[:, None])
    image_id = jnp.where(usable, holder[:, None], -1).reshape(-1)
    table_offset = jnp.where(holder_length == PATCH_BIG, 0, PATCH_BIG).astype(jnp.int32)
    position = jnp.where(usable, table_offset[:, None] + within, 0).reshape(-1)
    return (image_id, position)


def norm_unit(values):
    centre = jnp.mean(values, axis=-1, keepdims=True)
    centred = values - centre
    spread = jnp.mean(centred * centred, axis=-1, keepdims=True)
    return centred * lax.rsqrt(spread + eps_norm)


def norm_back(unit_rows, pull_unit, gain, grad_normed, row_weight):
    grad_values = pull_unit(grad_normed * gain)[0]
    weighted = grad_normed * row_weight[:, None]
    return (grad_values, jnp.sum(weighted * unit_rows, axis=0), jnp.sum(weighted, axis=0))


def gelu_exact(values):
    return jax.nn.gelu(values, approximate=False)


def split_heads(matrix):
    return matrix.reshape(matrix.shape[0], -1, DH)


def alternate(patch_part, special_part, groups):
    trailing = patch_part.shape[1:]
    joined = jnp.concatenate(
        [
            patch_part.reshape((groups, -1) + trailing),
            special_part.reshape((groups, -1) + trailing),
        ],
        axis=1,
    )
    return joined.reshape((-1,) + trailing)


def separate(combined, groups, quarter):
    trailing = combined.shape[1:]
    shaped = combined.reshape((groups, -1) + trailing)
    return (
        shaped[:, :quarter].reshape((-1,) + trailing),
        shaped[:, quarter:].reshape((-1,) + trailing),
    )


def empty_state(heads_local, query_count):
    return (
        jnp.full((heads_local, query_count), masked_score, jnp.float32),
        jnp.zeros((heads_local, query_count), jnp.float32),
        jnp.zeros((heads_local, query_count, DH), jnp.float32),
    )


def softmax_update(carried, queries, key_rows, value_rows, allowed, score_scale):
    running_top, running_total, running_sum = carried
    scores = (
        jnp.einsum("qhd,khd->hqk", queries, key_rows, preferred_element_type=jnp.float32)
        * score_scale
    )
    masked = jnp.where(allowed[None], scores, masked_score)
    new_top = jnp.maximum(running_top, jnp.max(masked, axis=-1))
    rescale = jnp.exp(running_top - new_top)
    weights = jnp.where(allowed[None], jnp.exp(masked - new_top[..., None]), 0.0)
    new_total = running_total * rescale + jnp.sum(weights, axis=-1)
    new_sum = running_sum * rescale[..., None] + jnp.einsum(
        "hqk,khd->hqd", weights.astype(jnp.bfloat16), value_rows, preferred_element_type=jnp.float32
    )
    return (new_top, new_total, new_sum)


def merge_softmax(first_part, second_part):
    joint_top = jnp.maximum(first_part[0], second_part[0])
    first_scale = jnp.exp(first_part[0] - joint_top)
    second_scale = jnp.exp(second_part[0] - joint_top)
    return (
        joint_top,
        first_part[1] * first_scale + second_part[1] * second_scale,
        first_part[2] * first_scale[..., None] + second_part[2] * second_scale[..., None],
    )


def finish_state(carried, usable):
    running_top, running_total, running_sum = carried
    safe_total = jnp.where(usable[None, :], running_total, 1.0)
    attended = running_sum / safe_total[..., None]
    log_total = jnp.where(usable[None, :], running_top + jnp.log(safe_total), 0.0)
    return (attended, log_total)


def pair_grads(queries, key_rows, value_rows, grad_attn, log_total, delta, allowed, score_scale):
    scores = (
        jnp.einsum("qhd,khd->hqk", queries, key_rows, preferred_element_type=jnp.float32)
        * score_scale
    )
    probs = jnp.where(
        allowed[None],
        jnp.exp(jnp.where(allowed[None], scores, masked_score) - log_total[..., None]),
        0.0,
    )
    grad_values = jnp.einsum(
        "hqk,qhd->khd", probs.astype(jnp.bfloat16), grad_attn, preferred_element_type=jnp.float32
    )
    grad_probs = jnp.einsum(
        "qhd,khd->hqk", grad_attn, value_rows, preferred_element_type=jnp.float32
    )
    grad_scores = (probs * (grad_probs - delta[..., None]) * score_scale).astype(jnp.bfloat16)
    grad_queries = jnp.einsum(
        "hqk,khd->qhd", grad_scores, key_rows, preferred_element_type=jnp.float32
    )
    grad_keys = jnp.einsum("hqk,qhd->khd", grad_scores, queries, preferred_element_type=jnp.float32)
    query_count = queries.shape[0]
    key_count = key_rows.shape[0]
    return (
        grad_queries.reshape(query_count, -1),
        grad_keys.reshape(key_count, -1),
        grad_values.reshape(key_count, -1),
    )


def on_device(
    patches,
    specials,
    pos_table,
    image_length,
    slot_band,
    w_qkv,
    qv_bias,
    w_out,
    branch_bias,
    ln_gain,
    ln_bias,
    layer_scale,
    w_up,
    up_bias,
    w_down,
    cot_patch,
    cot_special,
):
    seq_count = lax.axis_size("seq")
    tp_count = lax.axis_size("tp")
    seq_place = lax.axis_index("seq")
    tp_place = lax.axis_index("tp")
    quarter = patches.shape[0]
    spec_quarter = specials.shape[0]
    local_rows = quarter + spec_quarter
    seq_rows = quarter * tp_count
    spec_rows = spec_quarter * tp_count
    head_width = w_qkv.shape[2]
    heads_local = head_width // DH
    score_scale = DH ** (-0.5)
    image_all, position_all = band_layout(image_length, slot_band)
    seq_start = seq_place * seq_rows
    image_seq = lax.dynamic_slice_in_dim(image_all, seq_start, seq_rows)
    usable_seq = image_seq >= 0
    own_start = seq_start + tp_place * quarter
    image_mine = lax.dynamic_slice_in_dim(image_all, own_start, quarter)
    position_mine = lax.dynamic_slice_in_dim(position_all, own_start, quarter)
    usable_mine = (image_mine >= 0).astype(jnp.float32)
    special_image = jnp.arange(spec_rows, dtype=jnp.int32) // SPECIALS
    first_seq = (seq_place == 0).astype(jnp.float32)
    local_weight = jnp.concatenate(
        [jnp.ones((quarter,), jnp.float32), jnp.zeros((spec_quarter,), jnp.float32) + first_seq]
    )
    gathered_weight = jnp.tile(local_weight, tp_count).astype(jnp.bfloat16)
    placed = patches.astype(jnp.float32) + usable_mine[:, None] * pos_table[position_mine].astype(
        jnp.float32
    )
    stream = jnp.concatenate([placed, specials.astype(jnp.float32)], axis=0)
    unit_one, pull_one = jax.vjp(norm_unit, stream)
    normed = (unit_one * ln_gain[0] + ln_bias[0]).astype(jnp.bfloat16)
    normed_all = lax.all_gather(normed, "tp", axis=0, tiled=True)
    projected = jnp.einsum("nd,jdc->jnc", normed_all, w_qkv, preferred_element_type=jnp.float32)
    query_all = (projected[0] + qv_bias[0]).astype(jnp.bfloat16)
    key_all = projected[1].astype(jnp.bfloat16)
    value_all = (projected[2] + qv_bias[1]).astype(jnp.bfloat16)
    query_patch, query_spec = separate(query_all, tp_count, quarter)
    key_patch, key_spec = separate(key_all, tp_count, quarter)
    value_patch, value_spec = separate(value_all, tp_count, quarter)
    query_heads = split_heads(query_patch)
    key_heads = split_heads(key_patch)
    value_heads = split_heads(value_patch)
    spec_query_heads = split_heads(query_spec)
    key_spec_heads = split_heads(key_spec)
    value_spec_heads = split_heads(value_spec)
    allowed_ps = (image_seq[:, None] == special_image[None, :]) & usable_seq[:, None]
    allowed_sp = special_image[:, None] == image_seq[None, :]
    allowed_ss = special_image[:, None] == special_image[None, :]
    carried = softmax_update(
        empty_state(heads_local, seq_rows),
        query_heads,
        key_spec_heads,
        value_spec_heads,
        allowed_ps,
        score_scale,
    )
    pair_rows = jnp.concatenate([key_patch, value_patch], axis=1)
    portion = lax.all_gather(pair_rows, "seq", axis=0, tiled=True)
    portion_rows = portion.shape[0]
    block_rows = math.gcd(portion_rows, key_block)

    def one_block(block_turn, inner_state):
        offset = block_turn * block_rows
        visiting = lax.dynamic_slice_in_dim(portion, offset, block_rows, 0)
        visiting_image = lax.dynamic_slice_in_dim(image_all, offset, block_rows, 0)
        allowed = (image_seq[:, None] == visiting_image[None, :]) & usable_seq[:, None]
        return softmax_update(
            inner_state,
            query_heads,
            split_heads(visiting[:, :head_width]),
            split_heads(visiting[:, head_width:]),
            allowed,
            score_scale,
        )

    patch_state = lax.fori_loop(0, portion_rows // block_rows, one_block, carried)
    attended_patch, log_patch = finish_state(patch_state, usable_seq)
    partial_state = softmax_update(
        empty_state(heads_local, spec_rows),
        spec_query_heads,
        key_heads,
        value_heads,
        allowed_sp,
        score_scale,
    )
    merged_state = combined_all(partial_state, "seq", merge_softmax)
    special_state = softmax_update(
        merged_state, spec_query_heads, key_spec_heads, value_spec_heads, allowed_ss, score_scale
    )
    attended_spec, log_spec = finish_state(special_state, special_image >= 0)
    attn_patch_rows = jnp.transpose(attended_patch, (1, 0, 2)).reshape(seq_rows, head_width)
    attn_spec_rows = jnp.transpose(attended_spec, (1, 0, 2)).reshape(spec_rows, head_width)
    attn_all = alternate(
        attn_patch_rows.astype(jnp.bfloat16), attn_spec_rows.astype(jnp.bfloat16), tp_count
    )
    branch_one = lax.psum_scatter(
        jnp.dot(attn_all, w_out, preferred_element_type=jnp.float32).astype(jnp.bfloat16),
        "tp",
        scatter_dimension=0,
        tiled=True,
    ).astype(jnp.float32)
    mid_stream = stream + layer_scale[0] * (branch_one + branch_bias[0])
    unit_two, pull_two = jax.vjp(norm_unit, mid_stream)
    normed_two = (unit_two * ln_gain[1] + ln_bias[1]).astype(jnp.bfloat16)
    normed_two_all = lax.all_gather(normed_two, "tp", axis=0, tiled=True)
    hidden_pre = jnp.dot(normed_two_all, w_up, preferred_element_type=jnp.float32) + up_bias
    activated, pull_gelu = jax.vjp(gelu_exact, hidden_pre)
    hidden = activated.astype(jnp.bfloat16)
    branch_two = lax.psum_scatter(
        jnp.dot(hidden, w_down, preferred_element_type=jnp.float32).astype(jnp.bfloat16),
        "tp",
        scatter_dimension=0,
        tiled=True,
    ).astype(jnp.float32)
    result = mid_stream + layer_scale[1] * (branch_two + branch_bias[1])
    out_rows = result.astype(jnp.bfloat16)
    cotangent_all = alternate(cot_patch, cot_special, tp_count)
    grad_result = lax.dynamic_slice_in_dim(cotangent_all, tp_place * local_rows, local_rows).astype(
        jnp.float32
    )
    weighted_result = grad_result * local_weight[:, None]
    scale_grad_two = jnp.sum(weighted_result * (branch_two + branch_bias[1]), axis=0)
    bias_grad_two = jnp.sum(weighted_result, axis=0) * layer_scale[1]
    grad_two_all = (cotangent_all.astype(jnp.float32) * layer_scale[1]).astype(jnp.bfloat16)
    down_grad = jnp.einsum(
        "nf,nd->fd",
        hidden * gathered_weight[:, None],
        grad_two_all,
        preferred_element_type=jnp.float32,
    )
    grad_hidden = jnp.einsum("nd,fd->nf", grad_two_all, w_down, preferred_element_type=jnp.float32)
    grad_pre = pull_gelu(grad_hidden)[0].astype(jnp.bfloat16)
    up_grad = jnp.einsum(
        "nd,nf->df",
        normed_two_all * gathered_weight[:, None],
        grad_pre,
        preferred_element_type=jnp.float32,
    )
    up_bias_grad = jnp.dot(gathered_weight, grad_pre, preferred_element_type=jnp.float32)
    grad_normed_two = lax.psum_scatter(
        jnp.einsum("nf,df->nd", grad_pre, w_up, preferred_element_type=jnp.float32).astype(
            jnp.bfloat16
        ),
        "tp",
        scatter_dimension=0,
        tiled=True,
    ).astype(jnp.float32)
    grad_mid_norm, gain_grad_two, shift_grad_two = norm_back(
        unit_two, pull_two, ln_gain[1], grad_normed_two, local_weight
    )
    grad_mid = grad_result + grad_mid_norm
    weighted_mid = grad_mid * local_weight[:, None]
    scale_grad_one = jnp.sum(weighted_mid * (branch_one + branch_bias[0]), axis=0)
    bias_grad_one = jnp.sum(weighted_mid, axis=0) * layer_scale[0]
    grad_one = (grad_mid * layer_scale[0]).astype(jnp.bfloat16)
    grad_one_all = lax.all_gather(grad_one, "tp", axis=0, tiled=True)
    out_grad = jnp.einsum(
        "nc,nd->cd",
        attn_all * gathered_weight[:, None],
        grad_one_all,
        preferred_element_type=jnp.float32,
    )
    grad_attn_all = jnp.einsum(
        "nd,cd->nc", grad_one_all, w_out, preferred_element_type=jnp.float32
    ).astype(jnp.bfloat16)
    grad_attn_patch, grad_attn_spec = separate(grad_attn_all, tp_count, quarter)
    grad_attn_heads = split_heads(grad_attn_patch)
    spec_grad_heads = split_heads(grad_attn_spec)
    delta_patch = jnp.einsum("rhd,hrd->hr", grad_attn_heads.astype(jnp.float32), attended_patch)
    delta_spec = jnp.einsum("rhd,hrd->hr", spec_grad_heads.astype(jnp.float32), attended_spec)

    def key_turn(turn_count, cycle_state):
        visiting_pair, grad_pair, grad_query = cycle_state
        holder_seq = (seq_place - turn_count) % seq_count
        visiting_image = lax.dynamic_slice_in_dim(image_all, holder_seq * seq_rows, seq_rows)
        allowed = (image_seq[:, None] == visiting_image[None, :]) & usable_seq[:, None]
        query_part, key_part, value_part = pair_grads(
            query_heads,
            split_heads(visiting_pair[:, :head_width]),
            split_heads(visiting_pair[:, head_width:]),
            grad_attn_heads,
            log_patch,
            delta_patch,
            allowed,
            score_scale,
        )
        grad_query, grad_pair = (
            grad_query + query_part,
            grad_pair + jnp.concatenate([key_part, value_part], axis=1),
        )
        visiting_pair = shifted(visiting_pair, "seq", 1)
        grad_pair = shifted(grad_pair.astype(jnp.bfloat16), "seq", 1).astype(grad_pair.dtype)
        return (visiting_pair, grad_pair, grad_query)

    cycle_start = (
        pair_rows,
        jnp.zeros((seq_rows, 2 * head_width), jnp.float32),
        jnp.zeros((seq_rows, head_width), jnp.float32),
    )
    cycle_end = lax.fori_loop(0, seq_count, key_turn, cycle_start)
    grad_query_cycle = cycle_end[2]
    grad_pair_cycle = cycle_end[1]
    patch_spec_grads = pair_grads(
        query_heads,
        key_spec_heads,
        value_spec_heads,
        grad_attn_heads,
        log_patch,
        delta_patch,
        allowed_ps,
        score_scale,
    )
    spec_patch_grads = pair_grads(
        spec_query_heads,
        key_heads,
        value_heads,
        spec_grad_heads,
        log_spec,
        delta_spec,
        allowed_sp,
        score_scale,
    )
    summed_query, summed_key, summed_value = lax.psum(
        (spec_patch_grads[0], patch_spec_grads[1], patch_spec_grads[2]), "seq"
    )
    spec_spec_grads = pair_grads(
        spec_query_heads,
        key_spec_heads,
        value_spec_heads,
        spec_grad_heads,
        log_spec,
        delta_spec,
        allowed_ss,
        score_scale,
    )
    grad_query_rows = alternate(
        grad_query_cycle + patch_spec_grads[0], summed_query + spec_spec_grads[0], tp_count
    )
    grad_key_rows = alternate(
        grad_pair_cycle[:, :head_width] + spec_patch_grads[1],
        summed_key + spec_spec_grads[1],
        tp_count,
    )
    grad_value_rows = alternate(
        grad_pair_cycle[:, head_width:] + spec_patch_grads[2],
        summed_value + spec_spec_grads[2],
        tp_count,
    )
    grad_proj = jnp.stack([grad_query_rows, grad_key_rows, grad_value_rows]).astype(jnp.bfloat16)
    qkv_grad = jnp.einsum(
        "nd,jnc->jdc",
        normed_all * gathered_weight[:, None],
        grad_proj,
        preferred_element_type=jnp.float32,
    )
    qv_bias_grad = jnp.stack(
        [
            jnp.dot(gathered_weight, grad_proj[0], preferred_element_type=jnp.float32),
            jnp.dot(gathered_weight, grad_proj[2], preferred_element_type=jnp.float32),
        ]
    )
    grad_normed = lax.psum_scatter(
        jnp.einsum("jnc,jdc->nd", grad_proj, w_qkv, preferred_element_type=jnp.float32).astype(
            jnp.bfloat16
        ),
        "tp",
        scatter_dimension=0,
        tiled=True,
    ).astype(jnp.float32)
    grad_stream_norm, gain_grad_one, shift_grad_one = norm_back(
        unit_one, pull_one, ln_gain[0], grad_normed, local_weight
    )
    grad_stream = grad_mid + grad_stream_norm
    grad_patch_rows = grad_stream[:quarter]
    pos_grad = jax.ops.segment_sum(
        grad_patch_rows * usable_mine[:, None], position_mine, num_segments=pos_table.shape[0]
    )
    qkv_grad, qv_bias_grad, out_grad, up_grad, up_bias_grad, down_grad = lax.psum(
        (qkv_grad, qv_bias_grad, out_grad, up_grad, up_bias_grad, down_grad), "seq"
    )
    pos_grad, gain_grad, shift_grad, bias_grad, scale_grad = lax.psum(
        (
            pos_grad,
            jnp.stack([gain_grad_one, gain_grad_two]),
            jnp.stack([shift_grad_one, shift_grad_two]),
            jnp.stack([bias_grad_one, bias_grad_two]),
            jnp.stack([scale_grad_one, scale_grad_two]),
        ),
        ("seq", "tp"),
    )
    return (
        out_rows[:quarter],
        out_rows[quarter:],
        grad_patch_rows,
        grad_stream[quarter:],
        pos_grad,
        qkv_grad,
        qv_bias_grad,
        out_grad,
        bias_grad,
        gain_grad,
        shift_grad,
        scale_grad,
        up_grad,
        up_bias_grad,
        down_grad,
    )


def solution(mesh):
    in_specs = (
        P(("seq", "tp"), None),
        P("tp", None),
        P(),
        P(),
        P(),
        P(None, None, "tp"),
        P(None, "tp"),
        P("tp", None),
        P(),
        P(),
        P(),
        P(),
        P(None, "tp"),
        P("tp"),
        P("tp", None),
        P("seq", None),
        P(),
    )
    out_specs = (
        P(("seq", "tp"), None),
        P("tp", None),
        P(("seq", "tp"), None),
        P("tp", None),
        P(),
        P(None, None, "tp"),
        P(None, "tp"),
        P("tp", None),
        P(),
        P(),
        P(),
        P(),
        P(None, "tp"),
        P("tp"),
        P("tp", None),
    )
    return jax.shard_map(
        on_device, mesh=mesh, in_specs=in_specs, out_specs=out_specs, check_vma=False
    )
```

profile of v0, /device:TPU:0, one launch (start us, length us, event | category | flops | bytes accessed | tf_op | source)
XLA Modules:
  0.0 653.5 jit_solution(15331322480156954550)
XLA Ops:
  16.6 19.5 %all-gather.3 = bf16[4,101,768]{2,1,0:T(8,128)(2,1)S(1)} all-gather(bf16[1,101,768]{2,1,0:T(8,128)(2,1)S(1)} %fusion.77), channel_id=1, replica_groups=mesh['seq'=8,'tp'=4] {'tp'}, dimensions={0}, use_global_device_ids=true | all-gather | bytes 775680 | tf_op jit(solution)/shard_map/all_gather | solution.py:228
  42.7 8.9 %all-gather.4 = bf16[8,3,20]{2,1,0:T(4,128)(2,1)S(1)} all-gather(bf16[1,3,20]{2,1,0:T(4,128)(2,1)S(1)} %convert_bitcast_fusion.2), channel_id=2, replica_groups=mesh['seq'=8,'tp'=4] {'seq'}, dimensions={0}, use_global_device_ids=true | all-gather | bytes 1080 | tf_op jit(solution)/shard_map/all_gather | solution.py:21
  51.6 8.8 %all-gather.5 = bf16[8,3,20]{2,1,0:T(4,128)(2,1)S(1)} all-gather(bf16[1,3,20]{2,1,0:T(4,128)(2,1)S(1)} %get-tuple-element.823), channel_id=3, replica_groups=mesh['seq'=8,'tp'=4] {'seq'}, dimensions={0}, use_global_device_ids=true | all-gather | bytes 1080 | tf_op jit(solution)/shard_map/all_gather | solution.py:21
  60.7 8.5 %all-gather.2 = bf16[24,20,64]{2,1,0:T(8,128)(2,1)S(1)} all-gather(bf16[3,20,64]{2,1,0:T(8,128)(2,1)S(1)} %fusion.43), channel_id=4, replica_groups=mesh['seq'=8,'tp'=4] {'seq'}, dimensions={0}, use_global_device_ids=true | all-gather | bytes 69120 | tf_op jit(solution)/shard_map/all_gather | solution.py:21
  72.8 16.0 %while.56 = (s32[]{:T(128)}, f32[3,384]{1,0:T(4,128)S(1)}, f32[3,384]{1,0:T(4,128)S(1)}, f32[3,384,64]{1,2,0:T(8,128)S(1)}, s32[384]{0:T(512)S(1)}, /*index=5*/s...) while((s32[]{:T(128)}, f32[3,384]{1,0:T(4,128)S(1)}, ...), condition=%wide.region_12.13_spmd, body=%wide.region_9.12_spmd.sunk | while | flops 318261504 | bytes 18913356 | solution.py:272
  90.5 19.8 %fusion = bf16[104,768]{1,0:T(8,128)(2,1)S(1)} fusion(bf16[404,768]{1,0:T(8,128)(2,1)S(1)} %convolution_convert_fusion.2), kind=kCustom, calls=%all-reduce-scatter | all-reduce-scatter fusion | flops 319489 | bytes 780800
  115.7 15.9 %all-gather.6 = bf16[4,101,768]{2,1,0:T(8,128)(2,1)S(1)} all-gather(bf16[1,101,768]{2,1,0:T(8,128)(2,1)S(1)} %fusion.78), channel_id=1, replica_groups=mesh['seq'=8,'tp'=4] {'tp'}, dimensions={0}, use_global_device_ids=true | all-gather | bytes 775680 | tf_op jit(solution)/shard_map/all_gather | solution.py:301
  132.7 5.4 multiply_convert_fusion.2
  140.9 17.2 %fusion.2 = bf16[104,768]{1,0:T(8,128)(2,1)} fusion(bf16[404,768]{1,0:T(8,128)(2,1)} %convolution_convert_fusion), kind=kCustom, calls=%all-reduce-scatter.2 | all-reduce-scatter fusion | flops 319489 | bytes 780800
  158.8 2.2 collective-permute-start.4
  161.1 3.0 convolution_convert_fusion.1
  167.9 15.1 %all-gather.7 = bf16[4,101,768]{2,1,0:T(8,128)(2,1)S(1)} all-gather(bf16[1,101,768]{2,1,0:T(8,128)(2,1)S(1)} %get-tuple-element.793), channel_id=1, replica_groups=mesh['seq'=8,'tp'=4] {'tp'}, dimensions={0}, use_global_device_ids=true | all-gather | bytes 775680 | tf_op jit(solution)/shard_map/all_gather | solution.py:352
  194.4 22.9 %all-reduce.11 = (f32[20,192]{1,0:T(8,128)S(1)}, f32[20,192]{1,0:T(8,128)S(1)}) all-reduce(f32[20,192]{1,0:T(8,128)S(1)} %reshape.608, f32[20,192]{1,0:T(8,128)S(1)} %reshape.618), channel_id=1, replica_groups=mesh['seq'=8,'tp'=4] {'seq'}, use_global_device_ids=true, to_apply=%region_28.29 | all-reduce | flops 7680 | bytes 61440 | tf_op jit(solution)/shard_map/psum | solution.py:419
  217.6 86.9 %while.58 = (s32[]{:T(128)}, bf16[384,384]{0,1:T(8,128)(2,1)S(1)}, f32[384,384]{0,1:T(8,128)S(1)}, f32[384,192]{0,1:T(8,128)S(1)}, s32[384]{0:T(512)S(1)}, /*ind...) while((s32[]{:T(128)}, bf16[384,384]{0,1:T(8,128)(2,1)S(1)}, ...), condition=%wide.region_27.28_spmd.clone, body=%wide.region_26.27_spmd.clone.sunk | while | flops 288276480 | bytes 16973612 | solution.py:396
  221.9 6.5 collective-permute-done.1
  232.7 6.5 collective-permute-done.1
  243.6 6.5 collective-permute-done.1
  254.4 6.5 collective-permute-done.1
  265.3 6.5 collective-permute-done.1
  276.1 6.5 collective-permute-done.1
  287.0 6.5 collective-permute-done.1
  297.9 6.5 collective-permute-done.1
  308.6 22.5 %all-reduce.10 = (f32[20,192]{1,0:T(8,128)S(1)}, f32[2,192]{1,0:T(2,128)}, f32[768]{0:T(1024)}) all-reduce(f32[20,192]{1,0:T(8,128)S(1)} %reshape.613, f32[2,192]{1,0:T(2,128)S(1)} %pad_maximum_fusion.11, f32[768]{0:T(1024)S(1)} %copy-done.66), channel_id=1, replica_groups=mesh['seq'=8,'tp'=4] {'seq'}, use_global_device_ids=true, to_apply=%region_29.30 | all-reduce | flops 4992 | bytes 39936 | tf_op jit(solution)/shard_map/psum | solution.py:419
  334.3 25.5 %fusion.151 = (bf16[104,768]{1,0:T(8,128)(2,1)S(1)}, bf16[104,768]{1,0:T(8,128)(2,1)S(1)}) fusion(bf16[404,768]{1,0:T(8,128)(2,1)S(1)} %copy-done.32, bf16[404,768]{1,0:T(8,128)(2,1)} %fusion.24), kind=kCustom, calls=%all-reduce-scatter.4 | all-reduce-scatter fusion | flops 638977 | bytes 1561088
  361.2 2.7 collective-permute-start.3
  366.8 4.0 scatter_custom_fusion
  372.1 2.3 fusion.48
  374.4 2.3 fusion.46
  383.6 41.7 %all-reduce.9 = (f32[2,768]{1,0:T(2,128)}, f32[2,768]{1,0:T(2,128)}, f32[2,768]{1,0:T(2,128)}, f32[2,768]{1,0:T(2,128)}) all-reduce(f32[2,768]{1,0:T(2,128)S(1)} %pad_maximum_fusion.7, f32[2,768]{1,0:T(2,128)S(1)} %pad_maximum_fusion.8, f32[2,768]{1,0:T(2,128)S(1)} %pad_maximum_fusion.9, ...), channel_id=1, replica_groups=mesh['seq'=8,'tp'=4] {'seq','tp'}, use_global_device_ids=true, to_apply=%region_41.42 | all-reduce | flops 6144 | bytes 49152 | tf_op jit(solution)/shard_map/psum | solution.py:477
  425.3 91.9 %all-reduce.17.cloned.1.call-done = f32[1625,768]{1,0:T(8,128)} async-done(((f32[1625,768]{1,0:T(8,128)}), f32[1625,768]{1,0:T(8,128)}) %all-reduce.17.cloned.1.call-update) | async-done | bytes 4992016 | tf_op jit(solution)/shard_map/psum | solution.py:477
  517.2 118.0 %all-reduce.19.cloned.1.call-done = (f32[3,768,192]{1,2,0:T(8,128)}, f32[192,768]{1,0:T(8,128)}, f32[768,768]{1,0:T(8,128)}, f32[768,768]{1,0:T(8,128)}) async-done(((f32[3,768,192]{1,2,0:T(8,128)}, f32[192,768]{1,0:T(8,128)}, f32[768,768]{1,0:T(8,128)}, f32[768,768]{1,0:T(8,128)}), (f32[3,768,192]{1,2,0:T(8,128)}, f32[192,768]{1,0:T(8,128)}, f32[768,768]{1,0:T(8,128)}, ...) | async-done | bytes 7077904 | tf_op jit(solution)/shard_map/psum | solution.py:474
  635.2 5.2 copy.254
  (568 shorter events, 121.1 us)
Async XLA Ops:
  7.2 65.6 %all-gather.10.cloned.1.call-start = ((), (), s32[]{:S(2)}) async-start(), calls=%async_computation | async-start | bytes 2654208 | tf_op jit(solution)/shard_map/all_gather | solution.py:254
  39.7 477.4 %all-reduce.17.cloned.1.call-start = ((), (), s32[]{:S(2)}) async-start(), calls=%async_computation.1 | async-start | bytes 10027008 | tf_op jit(solution)/shard_map/psum | solution.py:477
  110.4 4.3 collective-permute-start.2
  112.4 53.8 %copy-start.78 = (f32[101]{0:T(128)}, f32[101]{0:T(128)S(1)}, u32[]{:S(2)}) copy-start(f32[101]{0:T(128)S(1)} %concatenate.44) | copy-start | bytes 1216
  113.1 50.9 %copy-start.57 = (bf16[404,1]{0,1:T(2,128)(2,1)}, bf16[404,1]{0,1:T(2,128)(2,1)S(1)}, u32[]{:S(2)}) copy-start(bf16[404,1]{0,1:T(2,128)(2,1)S(1)} %reshape.690) | copy-start | bytes 2428
  113.3 53.6 %copy-start.5 = (bf16[404,768]{1,0:T(8,128)(2,1)}, bf16[404,768]{1,0:T(8,128)(2,1)S(1)}, u32[]{:S(2)}) copy-start(bf16[404,768]{1,0:T(8,128)(2,1)S(1)} %reshape.604) | copy-start | bytes 1861636
  158.8 6.0 collective-permute-start.4
  217.6 10.8 %collective-permute-start = (bf16[384,384]{0,1:T(8,128)(2,1)S(1)}, bf16[384,384]{0,1:T(8,128)(2,1)S(1)}, u32[]{:S(2)}, u32[]{:S(2)}) collective-permute-start(bf16[384,384]{0,1:T(8,128)(2,1)S(1)} %copy.240), channel_id=1, source_target_pairs={{0,4},{4,8},{8,12},{12,16},{16,20},{20,24},{24,28},{28,0},{1,5},{5... | collective-permute-start | bytes 884744 | tf_op jit(solution)/shard_map/while/body/eval_jaxpr/ppermute | solution.py:40
  221.3 7.1 %collective-permute-start.1 = (bf16[384,384]{0,1:T(8,128)(2,1)S(1)}, bf16[384,384]{0,1:T(8,128)(2,1)S(1)}, u32[]{:S(2)}, u32[]{:S(2)}) collective-permute-start(bf16[384,384]{0,1:T(8,128)(2,1)S(1)} %fusion.268), channel_id=1, source_target_pairs={{0,4},{4,8},{8,12},{12,16},{16,20},{20,24},{24,28},{28,0},{1,5},{5... | collective-permute-start | bytes 884744 | tf_op jit(solution)/shard_map/while/body/eval_jaxpr/ppermute | solution.py:40
  228.5 10.8 %collective-permute-start = (bf16[384,384]{0,1:T(8,128)(2,1)S(1)}, bf16[384,384]{0,1:T(8,128)(2,1)S(1)}, u32[]{:S(2)}, u32[]{:S(2)}) collective-permute-start(bf16[384,384]{0,1:T(8,128)(2,1)S(1)} %copy.240), channel_id=1, source_target_pairs={{0,4},{4,8},{8,12},{12,16},{16,20},{20,24},{24,28},{28,0},{1,5},{5... | collective-permute-start | bytes 884744 | tf_op jit(solution)/shard_map/while/body/eval_jaxpr/ppermute | solution.py:40
  232.1 7.1 %collective-permute-start.1 = (bf16[384,384]{0,1:T(8,128)(2,1)S(1)}, bf16[384,384]{0,1:T(8,128)(2,1)S(1)}, u32[]{:S(2)}, u32[]{:S(2)}) collective-permute-start(bf16[384,384]{0,1:T(8,128)(2,1)S(1)} %fusion.268), channel_id=1, source_target_pairs={{0,4},{4,8},{8,12},{12,16},{16,20},{20,24},{24,28},{28,0},{1,5},{5... | collective-permute-start | bytes 884744 | tf_op jit(solution)/shard_map/while/body/eval_jaxpr/ppermute | solution.py:40
  239.3 10.8 %collective-permute-start = (bf16[384,384]{0,1:T(8,128)(2,1)S(1)}, bf16[384,384]{0,1:T(8,128)(2,1)S(1)}, u32[]{:S(2)}, u32[]{:S(2)}) collective-permute-start(bf16[384,384]{0,1:T(8,128)(2,1)S(1)} %copy.240), channel_id=1, source_target_pairs={{0,4},{4,8},{8,12},{12,16},{16,20},{20,24},{24,28},{28,0},{1,5},{5... | collective-permute-start | bytes 884744 | tf_op jit(solution)/shard_map/while/body/eval_jaxpr/ppermute | solution.py:40
  243.0 7.1 %collective-permute-start.1 = (bf16[384,384]{0,1:T(8,128)(2,1)S(1)}, bf16[384,384]{0,1:T(8,128)(2,1)S(1)}, u32[]{:S(2)}, u32[]{:S(2)}) collective-permute-start(bf16[384,384]{0,1:T(8,128)(2,1)S(1)} %fusion.268), channel_id=1, source_target_pairs={{0,4},{4,8},{8,12},{12,16},{16,20},{20,24},{24,28},{28,0},{1,5},{5... | collective-permute-start | bytes 884744 | tf_op jit(solution)/shard_map/while/body/eval_jaxpr/ppermute | solution.py:40
  250.2 10.8 %collective-permute-start = (bf16[384,384]{0,1:T(8,128)(2,1)S(1)}, bf16[384,384]{0,1:T(8,128)(2,1)S(1)}, u32[]{:S(2)}, u32[]{:S(2)}) collective-permute-start(bf16[384,384]{0,1:T(8,128)(2,1)S(1)} %copy.240), channel_id=1, source_target_pairs={{0,4},{4,8},{8,12},{12,16},{16,20},{20,24},{24,28},{28,0},{1,5},{5... | collective-permute-start | bytes 884744 | tf_op jit(solution)/shard_map/while/body/eval_jaxpr/ppermute | solution.py:40
  253.8 7.1 %collective-permute-start.1 = (bf16[384,384]{0,1:T(8,128)(2,1)S(1)}, bf16[384,384]{0,1:T(8,128)(2,1)S(1)}, u32[]{:S(2)}, u32[]{:S(2)}) collective-permute-start(bf16[384,384]{0,1:T(8,128)(2,1)S(1)} %fusion.268), channel_id=1, source_target_pairs={{0,4},{4,8},{8,12},{12,16},{16,20},{20,24},{24,28},{28,0},{1,5},{5... | collective-permute-start | bytes 884744 | tf_op jit(solution)/shard_map/while/body/eval_jaxpr/ppermute | solution.py:40
  261.1 10.8 %collective-permute-start = (bf16[384,384]{0,1:T(8,128)(2,1)S(1)}, bf16[384,384]{0,1:T(8,128)(2,1)S(1)}, u32[]{:S(2)}, u32[]{:S(2)}) collective-permute-start(bf16[384,384]{0,1:T(8,128)(2,1)S(1)} %copy.240), channel_id=1, source_target_pairs={{0,4},{4,8},{8,12},{12,16},{16,20},{20,24},{24,28},{28,0},{1,5},{5... | collective-permute-start | bytes 884744 | tf_op jit(solution)/shard_map/while/body/eval_jaxpr/ppermute | solution.py:40
  264.7 7.1 %collective-permute-start.1 = (bf16[384,384]{0,1:T(8,128)(2,1)S(1)}, bf16[384,384]{0,1:T(8,128)(2,1)S(1)}, u32[]{:S(2)}, u32[]{:S(2)}) collective-permute-start(bf16[384,384]{0,1:T(8,128)(2,1)S(1)} %fusion.268), channel_id=1, source_target_pairs={{0,4},{4,8},{8,12},{12,16},{16,20},{20,24},{24,28},{28,0},{1,5},{5... | collective-permute-start | bytes 884744 | tf_op jit(solution)/shard_map/while/body/eval_jaxpr/ppermute | solution.py:40
  271.9 10.8 %collective-permute-start = (bf16[384,384]{0,1:T(8,128)(2,1)S(1)}, bf16[384,384]{0,1:T(8,128)(2,1)S(1)}, u32[]{:S(2)}, u32[]{:S(2)}) collective-permute-start(bf16[384,384]{0,1:T(8,128)(2,1)S(1)} %copy.240), channel_id=1, source_target_pairs={{0,4},{4,8},{8,12},{12,16},{16,20},{20,24},{24,28},{28,0},{1,5},{5... | collective-permute-start | bytes 884744 | tf_op jit(solution)/shard_map/while/body/eval_jaxpr/ppermute | solution.py:40
  275.6 7.1 %collective-permute-start.1 = (bf16[384,384]{0,1:T(8,128)(2,1)S(1)}, bf16[384,384]{0,1:T(8,128)(2,1)S(1)}, u32[]{:S(2)}, u32[]{:S(2)}) collective-permute-start(bf16[384,384]{0,1:T(8,128)(2,1)S(1)} %fusion.268), channel_id=1, source_target_pairs={{0,4},{4,8},{8,12},{12,16},{16,20},{20,24},{24,28},{28,0},{1,5},{5... | collective-permute-start | bytes 884744 | tf_op jit(solution)/shard_map/while/body/eval_jaxpr/ppermute | solution.py:40
  282.8 10.8 %collective-permute-start = (bf16[384,384]{0,1:T(8,128)(2,1)S(1)}, bf16[384,384]{0,1:T(8,128)(2,1)S(1)}, u32[]{:S(2)}, u32[]{:S(2)}) collective-permute-start(bf16[384,384]{0,1:T(8,128)(2,1)S(1)} %copy.240), channel_id=1, source_target_pairs={{0,4},{4,8},{8,12},{12,16},{16,20},{20,24},{24,28},{28,0},{1,5},{5... | collective-permute-start | bytes 884744 | tf_op jit(solution)/shard_map/while/body/eval_jaxpr/ppermute | solution.py:40
  286.4 7.1 %collective-permute-start.1 = (bf16[384,384]{0,1:T(8,128)(2,1)S(1)}, bf16[384,384]{0,1:T(8,128)(2,1)S(1)}, u32[]{:S(2)}, u32[]{:S(2)}) collective-permute-start(bf16[384,384]{0,1:T(8,128)(2,1)S(1)} %fusion.268), channel_id=1, source_target_pairs={{0,4},{4,8},{8,12},{12,16},{16,20},{20,24},{24,28},{28,0},{1,5},{5... | collective-permute-start | bytes 884744 | tf_op jit(solution)/shard_map/while/body/eval_jaxpr/ppermute | solution.py:40
  293.6 10.8 %collective-permute-start = (bf16[384,384]{0,1:T(8,128)(2,1)S(1)}, bf16[384,384]{0,1:T(8,128)(2,1)S(1)}, u32[]{:S(2)}, u32[]{:S(2)}) collective-permute-start(bf16[384,384]{0,1:T(8,128)(2,1)S(1)} %copy.240), channel_id=1, source_target_pairs={{0,4},{4,8},{8,12},{12,16},{16,20},{20,24},{24,28},{28,0},{1,5},{5... | collective-permute-start | bytes 884744 | tf_op jit(solution)/shard_map/while/body/eval_jaxpr/ppermute | solution.py:40
  297.3 7.1 %collective-permute-start.1 = (bf16[384,384]{0,1:T(8,128)(2,1)S(1)}, bf16[384,384]{0,1:T(8,128)(2,1)S(1)}, u32[]{:S(2)}, u32[]{:S(2)}) collective-permute-start(bf16[384,384]{0,1:T(8,128)(2,1)S(1)} %fusion.268), channel_id=1, source_target_pairs={{0,4},{4,8},{8,12},{12,16},{16,20},{20,24},{24,28},{28,0},{1,5},{5... | collective-permute-start | bytes 884744 | tf_op jit(solution)/shard_map/while/body/eval_jaxpr/ppermute | solution.py:40
  334.2 31.4 %copy-start.51 = (f32[768]{0:T(1024)S(1)}, f32[768]{0:T(1024)}, u32[]{:S(2)}) copy-start(f32[768]{0:T(1024)} %copy-done.50) | copy-start | bytes 9220
  334.2 31.4 %copy-start.53 = (f32[768]{0:T(1024)S(1)}, f32[768]{0:T(1024)}, u32[]{:S(2)}) copy-start(f32[768]{0:T(1024)} %copy-done.52) | copy-start | bytes 9220
  334.3 31.4 %copy-start.55 = (f32[768]{0:T(1024)S(1)}, f32[768]{0:T(1024)}, u32[]{:S(2)}) copy-start(f32[768]{0:T(1024)} %copy-done.54) | copy-start | bytes 9220
  334.3 31.4 %copy-start.64 = (f32[768]{0:T(1024)S(1)}, f32[768]{0:T(1024)}, u32[]{:S(2)}) copy-start(f32[768]{0:T(1024)} %get-tuple-element.700) | copy-start | bytes 9220
  334.3 31.4 %copy-start.70 = (f32[101]{0:T(128)S(1)}, f32[101]{0:T(128)}, u32[]{:S(2)}) copy-start(f32[101]{0:T(128)} %copy-done.69) | copy-start | bytes 1216
  334.3 31.4 %copy-start.75 = (f32[101]{0:T(128)S(1)}, f32[101]{0:T(128)}, u32[]{:S(2)}) copy-start(f32[101]{0:T(128)} %copy-done.74) | copy-start | bytes 1216
  359.8 4.0 collective-permute-start.5
  361.2 4.2 collective-permute-start.3
  370.8 264.3 %all-reduce.19.cloned.1.call-start = ((), (), s32[]{:S(2)}) async-start(), calls=%async_computation.2 | async-start | bytes 14155776 | tf_op jit(solution)/shard_map/psum | solution.py:474
  (83 other events, 702.6 us)
Sparse Core Ops, SparseCore 0:
  39.9 30.3 all-gather.9
  371.0 146.1 all-reduce.16
  522.5 112.6 all-reduce.18
where the time goes:
time: 655 us; the launch traced here: 653 us
  waiting for transfers between devices  263 us (40%)
  blocking collectives  226 us (35%)
  matrix products  63.2 us (10%)
  local copies, waits for them, and re-layouts  45.1 us (7%)
  other arithmetic  28.7 us (4%)
  between operations  16.1 us (2%)
  starting transfers between devices  8.86 us (1%)
    psum x1, waiting for transfers between devices, on_device(): lax.psum((qkv_grad, qv_bias_grad, out_grad, up_grad, up_bias_grad, down_g...  118 us
    psum x1, waiting for transfers between devices, on_device(): lax.psum((pos_grad, jnp.stack([gain_grad_one, gain_grad_two]), jnp.stack(...  91.9 us
    unnamed x3, blocking collectives  62.5 us
    ppermute x16, waiting for transfers between devices, shifted(): lax.ppermute(value, axis, [(i, (i + by) % peers) for i in range(peers)])  52.3 us
    psum x2, blocking collectives, on_device(): lax.psum((spec_patch_grads[0], patch_spec_grads[1], patch_spec_grads[2]),...  45.5 us
    psum x1, blocking collectives, on_device(): lax.psum((pos_grad, jnp.stack([gain_grad_one, gain_grad_two]), jnp.stack(...  41.7 us
    all_gather x3, blocking collectives, combined_all(): lax.all_gather(a.astype(kind), axis)  26.2 us
    unnamed x203, local copies, waits for them, and re-layouts  23 us
  transfers between devices with their start and end apart: 23, of which 11 were waited for; matrix products, arithmetic and copies ran while one was open for 8% of the time, Pallas kernels for 0%

commit v1 on v0

v1 whole, which is shorter than its diff:
```python
import functools

import jax
import jax.numpy as jnp
from jax import lax
from jax.experimental import pallas as pl
from jax.experimental.pallas import tpu as pltpu
from jax.sharding import PartitionSpec as P

DH = 64
SPECIALS = 5
PATCH_BIG = 1369
BAND = 64

GROUP = 16
LANES = 256
FAR = 1e30
EPS = 1e-06
BIG_BANDS = (PATCH_BIG + BAND - 1) // BAND
WINDOW = -(-(BIG_BANDS + 1) * BAND // 256) * 256
VMEM_LIMIT = 60 * 1024 * 1024

bf16 = jnp.bfloat16
f32 = jnp.float32


def dot(a, b):
    return jnp.dot(a, b, preferred_element_type=f32)


def dot_nt(a, b):
    return lax.dot_general(a, b, (((1,), (1,)), ((), ())), preferred_element_type=f32)


def dot_tn(a, b):
    return lax.dot_general(a, b, (((0,), (0,)), ((), ())), preferred_element_type=f32)


def lanes_of(shape):
    return lax.broadcasted_iota(jnp.int32, shape, len(shape) - 1)


def norm_parts(values):
    centre = jnp.mean(values, axis=-1, keepdims=True)
    centred = values - centre
    spread = jnp.mean(centred * centred, axis=-1, keepdims=True)
    scale = lax.rsqrt(spread + EPS)
    return centred * scale, scale


def norm_back(unit, scale, eg):
    first = jnp.mean(eg, axis=-1, keepdims=True)
    second = jnp.mean(eg * unit, axis=-1, keepdims=True)
    return scale * (eg - first - unit * second)


def key_head(lane, h):
    return (lane >= h * DH) & (lane < (h + 1) * DH)


def value_head(lane, h):
    start = (0, DH, 3 * DH)[h]
    return (lane >= start) & (lane < start + DH)


def key_side(lane, h, images):
    image_lane = (lane >= 3 * DH) & (lane <= 3 * DH + images)
    lse_start = 3 * DH + images + 1 + 3 * h
    return key_head(lane, h) | image_lane | ((lane >= lse_start) & (lane < lse_start + 3))


def value_side(lane, h):
    start = 2 * DH + 3 * h
    return value_head(lane, h) | ((lane >= start) & (lane < start + 3))


def three_pieces(x):
    high = x.astype(bf16).astype(f32)
    rest = x - high
    middle = rest.astype(bf16).astype(f32)
    return high, middle, (rest - middle).astype(bf16).astype(f32)


def stacked(rows, picks):
    zero = jnp.zeros_like(rows)
    return jnp.concatenate([jnp.where(pick, rows, zero) for pick in picks], axis=0)


def spread_sum(stack, picks):
    count = stack.shape[0] // len(picks)
    total = None
    for h, pick in enumerate(picks):
        part = jnp.where(pick, stack[h * count : (h + 1) * count], 0.0)
        total = part if total is None else total + part
    return total


def call(body, outs, ins, scratch=(), outside=()):
    spaces = []
    for i, item in enumerate(ins):
        smem = item.dtype == jnp.int32 and item.ndim == 1
        space = pl.ANY if i in outside else pltpu.SMEM if smem else pltpu.VMEM
        spaces.append(pl.BlockSpec(memory_space=space))
    return pl.pallas_call(
        body,
        out_shape=[jax.ShapeDtypeStruct(s, d) for s, d in outs],
        in_specs=spaces,
        out_specs=[pl.BlockSpec(memory_space=pltpu.VMEM) for _ in outs],
        scratch_shapes=list(scratch),
        compiler_params=pltpu.CompilerParams(vmem_limit_bytes=VMEM_LIMIT),
    )(*ins)


def for_each(count, body):
    if count <= 8:
        for i in range(count):
            body(i)
    else:

        def step(i, carry):
            body(i)
            return carry

        lax.fori_loop(0, count, step, 0)


def embed_kernel(sizes, place, *refs):
    tp_count, quarter, special, images = sizes
    xs = refs[:tp_count]
    pos, w_cat, b_cat, gain, shift, row_image = refs[tp_count : tp_count + 6]
    stream, own, normed, query, pack, key_own, value_own = refs[tp_count + 6 :]
    rows = quarter * tp_count
    me = place[0]
    for k in range(tp_count):
        spot = lax.rem(me - k + tp_count, tp_count)
        patch_at = pl.multiple_of(spot * quarter, 16)
        special_at = pl.multiple_of(rows + spot * special, 16)
        part = xs[k][:quarter].astype(f32) + pos[pl.ds(patch_at, quarter)].astype(f32)
        stream[pl.ds(patch_at, quarter)] = part
        tail = xs[k][quarter:].astype(f32)
        stream[pl.ds(special_at, special)] = tail
        if k == 0:
            own[:quarter] = part
            own[quarter:] = tail
    unit, _ = norm_parts(stream[...])
    rounded = (unit * gain[...] + shift[...]).astype(bf16)
    normed[...] = rounded
    projected = (dot(rounded, w_cat[...]) + b_cat[...]).astype(bf16)
    image = row_image[...]
    total = image.shape[0]
    lane = lanes_of((total, LANES))
    image_lane = (lane >= 3 * DH) & (lane <= 3 * DH + images)
    scaled = projected[:, :LANES].astype(f32) * (DH**-0.5)
    far = jnp.where(image_lane & (lane != 3 * DH + image), FAR, 0.0)
    query[...] = jnp.where(lane < 3 * DH, scaled, far).astype(bf16)
    pack[...] = projected[:, LANES:]
    own_lane = 3 * DH + jnp.where(image < 0, images, image)
    lse_lane = (lane > 3 * DH + images) & (lane <= 3 * DH + images + 9)
    aux = jnp.where((lane == own_lane) | lse_lane, -1.0, 0.0)
    key_own[...] = jnp.where(
        lane < 3 * DH, projected[:, LANES : 2 * LANES].astype(f32), aux
    ).astype(bf16)
    half = lanes_of((total, 128))
    value_own[:, :128] = projected[:, 512:640]
    value_own[:, 128:] = jnp.where(
        half < DH,
        jnp.where(half < 9, -1.0, 0.0),
        projected[:, 384:512].astype(f32),
    ).astype(bf16)


def attend_kernel(sizes, slots, windows, *refs):
    blocks_count, bands, images, rows = sizes
    blocks = refs[:blocks_count]
    key_own, value_own, query = refs[blocks_count : blocks_count + 3]
    keys, values, attended, attended_b, query_out = refs[blocks_count + 3 :]
    lane = lanes_of((1, LANES))
    lse_lane = (lane > 3 * DH + images) & (lane <= 3 * DH + images + 9)
    empty = jnp.where((lane == 3 * DH + images) | lse_lane, -1.0, 0.0)
    buffer_rows = keys.shape[0]

    def clear(i, carry):
        at = pl.multiple_of(i * BAND, BAND)
        keys[pl.ds(at, BAND)] = jnp.broadcast_to(empty, (BAND, LANES)).astype(bf16)
        values[pl.ds(at, BAND)] = jnp.zeros((BAND, LANES), bf16)
        return carry

    lax.fori_loop(0, buffer_rows // BAND, clear, 0)
    band_lane = lanes_of((BAND, LANES))
    half = lanes_of((BAND, 128))
    in_band = lax.broadcasted_iota(jnp.int32, (BAND, LANES), 0)
    band_lse = (band_lane > 3 * DH + images) & (band_lane <= 3 * DH + images + 9)
    delta_aux = jnp.where(half < 9, -1.0, 0.0)
    per_block = blocks[0].shape[0] // BAND
    slot_count = blocks_count * per_block
    for b in range(blocks_count):

        def place(j, b=b):
            slot = b * per_block + j
            valid = slots[2 * slot_count + slot]

            @pl.when(valid > 0)
            def _():
                at = pl.multiple_of(slots[slot], BAND)
                image = slots[slot_count + slot]
                source = blocks[b][pl.ds(pl.multiple_of(j * BAND, BAND), BAND)]
                own_lane = 3 * DH + jnp.where(in_band < valid, image, images)
                aux = jnp.where((band_lane == own_lane) | band_lse, -1.0, 0.0)
                keys[pl.ds(at, BAND)] = jnp.where(
                    band_lane < 3 * DH, source[:, :LANES].astype(f32), aux
                ).astype(bf16)
                values[pl.ds(at, BAND), :128] = source[:, 256:384]
                values[pl.ds(at, BAND), 128:] = jnp.where(
                    half < DH, delta_aux, source[:, 128:256].astype(f32)
                ).astype(bf16)

        for_each(per_block, place)

    def place_special(i):
        at = pl.multiple_of(windows[bands + i], BAND)
        source = pl.ds(pl.multiple_of(rows + i * GROUP, GROUP), GROUP)
        keys[pl.ds(at, GROUP)] = key_own[source]
        values[pl.ds(at, GROUP)] = value_own[source]

    for_each(images, place_special)
    key_picks = [key_side(lane, h, images) for h in range(3)]
    value_picks = [value_head(lane, h) for h in range(3)]

    def unit(window, start, count):
        at = pl.multiple_of(windows[window], BAND)
        spot = pl.ds(start, count)
        own = query[spot]
        key_part = keys[pl.ds(at, WINDOW)]
        value_part = values[pl.ds(at, WINDOW)]
        scores = dot_nt(stacked(own, key_picks), key_part)
        top = jnp.maximum(jnp.max(scores, axis=-1, keepdims=True), -0.1 * FAR)
        weights = jnp.exp(scores - top)
        total = jnp.sum(weights, axis=-1, keepdims=True)
        usable = total > 0.0
        safe = jnp.where(usable, total, 1.0)
        summed = dot(weights.astype(bf16), value_part) / safe
        result = spread_sum(summed, value_picks)
        attended[spot] = result
        attended_b[spot] = result.astype(bf16)
        lse = jnp.where(usable, top + jnp.log(safe), 0.0)
        row = own.astype(f32)
        for h in range(3):
            for piece, part in enumerate(three_pieces(lse[h * count : (h + 1) * count])):
                row = jnp.where(lane == 3 * DH + images + 1 + 3 * h + piece, part, row)
        query_out[spot] = row.astype(bf16)

    for u in range(bands):
        unit(u, u * BAND, BAND)
    for_each(
        images,
        lambda i: unit(bands + i, pl.multiple_of(rows + i * GROUP, GROUP), GROUP),
    )


def feed_kernel(sizes, place, *refs):
    tp_count, quarter, special = sizes
    attended = refs[:tp_count]
    w_outs = refs[tp_count : 2 * tp_count]
    (stream, scale, bias, gain, shift, w_up, up_bias, grad_hidden) = refs[
        2 * tp_count : 2 * tp_count + 8
    ]
    mid_own, one_own, normed, hidden_out, grad_pre_out = refs[2 * tp_count + 8 : 2 * tp_count + 13]
    parts = refs[2 * tp_count + 13 : 3 * tp_count + 13]
    mid, partial = refs[3 * tp_count + 13 :]
    rows = quarter * tp_count
    me = place[0]
    one = dot(attended[0][...], w_outs[0][...])
    for k in range(1, tp_count):
        one += dot(attended[k][...], w_outs[k][...])
    partial[...] = one
    value = stream[...] + scale[0:1] * (one + bias[0:1])
    mid[...] = value
    own_patch = pl.ds(pl.multiple_of(me * quarter, 16), quarter)
    own_special = pl.ds(pl.multiple_of(rows + me * special, 16), special)
    mid_own[:quarter] = mid[own_patch]
    mid_own[quarter:] = mid[own_special]
    one_own[:quarter] = partial[own_patch]
    one_own[quarter:] = partial[own_special]
    unit, _ = norm_parts(value)
    rounded = (unit * gain[...] + shift[...]).astype(bf16)
    normed[...] = rounded
    pre = dot(rounded, w_up[...]) + up_bias[...]
    share = 0.5 * (1.0 + lax.erf(pre * (0.5**0.5)))
    hidden_out[...] = (pre * share).astype(bf16)
    slope = share + pre * jnp.exp(-0.5 * pre * pre) * (0.5 / jnp.pi) ** 0.5
    grad_pre = (grad_hidden[...] * slope).astype(bf16)
    grad_pre_out[...] = grad_pre
    partial[...] = dot_nt(grad_pre, w_up[...])
    send_blocks(me, parts, partial, quarter, special)


def send_blocks(me, parts, partial, quarter, special):
    tp_count = len(parts)
    rows = quarter * tp_count
    for k in range(tp_count):
        spot = lax.rem(me + k, tp_count)
        patch_at = pl.ds(pl.multiple_of(spot * quarter, 16), quarter)
        special_at = pl.ds(pl.multiple_of(rows + spot * special, 16), special)
        parts[k][:quarter] = partial[patch_at].astype(parts[k].dtype)
        parts[k][quarter:] = partial[special_at].astype(parts[k].dtype)


def mid_back_kernel(tp_count, *refs):
    parts = refs[:tp_count]
    mid, one, grad_result, weight, scale, bias, gain = refs[tp_count : tp_count + 7]
    w_outs = refs[tp_count + 7 : 2 * tp_count + 7]
    grad_mid_out, grad_one_out, small = refs[2 * tp_count + 7 : 2 * tp_count + 10]
    sends = refs[2 * tp_count + 10 :]
    incoming = parts[0][...]
    for k in range(1, tp_count):
        incoming += parts[k][...].astype(f32)
    unit, scaling = norm_parts(mid[...])
    grad_mid = grad_result[...] + norm_back(unit, scaling, incoming * gain[...])
    weighted = incoming * weight[...]
    weighted_mid = grad_mid * weight[...]
    small[0:1] = jnp.sum(weighted * unit, axis=0, keepdims=True)
    small[1:2] = jnp.sum(weighted, axis=0, keepdims=True)
    small[2:3] = jnp.sum(weighted_mid * (one[...] + bias[0:1]), axis=0, keepdims=True)
    small[3:4] = jnp.sum(weighted_mid, axis=0, keepdims=True) * scale[0:1]
    small[4:8] = jnp.zeros((4, small.shape[1]), f32)
    grad_mid_out[...] = grad_mid
    grad_one = (grad_mid * scale[0:1]).astype(bf16)
    grad_one_out[...] = grad_one
    for k in range(tp_count):
        sends[k][...] = dot_nt(grad_one, w_outs[(tp_count - k) % tp_count][...]).astype(bf16)


def delta_kernel(sizes, place, *refs):
    tp_count, quarter, special = sizes
    parts = refs[:tp_count]
    attended, out, whole = refs[tp_count:]
    rows = quarter * tp_count
    me = place[0]
    for k in range(tp_count):
        spot = lax.rem(me - k + tp_count, tp_count)
        whole[pl.ds(pl.multiple_of(spot * quarter, 16), quarter)] = parts[k][:quarter].astype(f32)
        whole[pl.ds(pl.multiple_of(rows + spot * special, 16), special)] = parts[k][
            quarter:
        ].astype(f32)
    value = whole[...]
    product = value * attended[...]
    lane = lanes_of(value.shape)
    for h in range(3):
        delta = jnp.sum(jnp.where(value_head(lane, h), product, 0.0), axis=-1, keepdims=True)
        for piece, part in enumerate(three_pieces(delta)):
            value = jnp.where(lane == 2 * DH + 3 * h + piece, part, value)
    out[...] = value.astype(bf16)


def query_grad_kernel(sizes, windows, query, grad, keys, values, out):
    bands, images, rows = sizes
    lane = lanes_of((1, LANES))
    key_picks = [key_side(lane, h, images) for h in range(3)]
    value_picks = [value_side(lane, h) for h in range(3)]
    head_picks = [key_head(lane, h) for h in range(3)]

    def unit(window, start, count):
        at = pl.multiple_of(windows[window], BAND)
        spot = pl.ds(start, count)
        key_part = keys[pl.ds(at, WINDOW)]
        probs = jnp.exp(dot_nt(stacked(query[spot], key_picks), key_part))
        pulled = dot_nt(stacked(grad[spot], value_picks), values[pl.ds(at, WINDOW)])
        scores = (probs * pulled).astype(bf16)
        result = spread_sum(dot(scores, key_part), head_picks) * DH**-0.5
        out[spot] = result.astype(bf16)

    for u in range(bands):
        unit(u, u * BAND, BAND)
    for_each(
        images,
        lambda i: unit(bands + i, pl.multiple_of(rows + i * GROUP, GROUP), GROUP),
    )


def pair_grad_kernel(sizes, place, slots, windows, *refs):
    blocks_count, bands, images, tp_count, quarter, special = sizes
    query_blocks = refs[:blocks_count]
    grad_blocks = refs[blocks_count : 2 * blocks_count]
    rest = refs[2 * blocks_count :]
    query_own, grad_own, key_own, value_own, grad_query, w_cat, joined = rest[:7]
    parts = rest[7 : 7 + tp_count]
    queries, grads, partial = rest[7 + tp_count :]
    rows = quarter * tp_count
    lane = lanes_of((1, LANES))
    image_lane = (lane >= 3 * DH) & (lane <= 3 * DH + images)
    empty = jnp.where(image_lane, FAR, 0.0)

    def clear(i, carry):
        at = pl.multiple_of(i * BAND, BAND)
        queries[pl.ds(at, BAND)] = jnp.broadcast_to(empty, (BAND, LANES)).astype(bf16)
        grads[pl.ds(at, BAND)] = jnp.zeros((BAND, LANES), bf16)
        return carry

    lax.fori_loop(0, queries.shape[0] // BAND, clear, 0)
    per_block = query_blocks[0].shape[0] // BAND
    slot_count = blocks_count * per_block
    for b in range(blocks_count):

        def put(j, b=b):
            slot = b * per_block + j

            @pl.when(slots[2 * slot_count + slot] > 0)
            def _():
                at = pl.multiple_of(slots[slot], BAND)
                source = pl.ds(pl.multiple_of(j * BAND, BAND), BAND)
                if blocks_count == 1:
                    pltpu.sync_copy(query_blocks[b].at[source], queries.at[pl.ds(at, BAND)])
                    pltpu.sync_copy(grad_blocks[b].at[source], grads.at[pl.ds(at, BAND)])
                else:
                    queries[pl.ds(at, BAND)] = query_blocks[b][source]
                    grads[pl.ds(at, BAND)] = grad_blocks[b][source]

        for_each(per_block, put)

    def put_special(i):
        at = pl.multiple_of(windows[bands + i], BAND)
        source = pl.ds(pl.multiple_of(rows + i * GROUP, GROUP), GROUP)
        queries[pl.ds(at, GROUP)] = query_own[source]
        grads[pl.ds(at, GROUP)] = grad_own[source]

    for_each(images, put_special)
    key_picks = [key_side(lane, h, images) for h in range(3)]
    value_picks = [value_side(lane, h) for h in range(3)]
    key_heads = [key_head(lane, h) for h in range(3)]
    value_heads = [value_head(lane, h) for h in range(3)]

    def unit(window, start, count):
        at = pl.multiple_of(windows[window], BAND)
        spot = pl.ds(start, count)
        query_part = queries[pl.ds(at, WINDOW)]
        grad_part = grads[pl.ds(at, WINDOW)]
        probs = jnp.exp(dot_nt(stacked(key_own[spot], key_picks), query_part))
        pulled = dot_nt(stacked(value_own[spot], value_picks), grad_part)
        scores = (probs * pulled).astype(bf16)
        grad_key = spread_sum(dot(scores, query_part), key_heads)
        grad_value = spread_sum(dot(probs.astype(bf16), grad_part), value_heads)
        joined[spot, 256:384] = grad_key[:, :128].astype(bf16)
        half = lanes_of((count, 128))
        joined[spot, 384:512] = jnp.where(half < DH, grad_key[:, 128:], grad_value[:, 128:]).astype(
            bf16
        )
        joined[spot, 512:640] = grad_value[:, :128].astype(bf16)

    joined[:, :256] = grad_query[...]
    for u in range(bands):
        unit(u, u * BAND, BAND)
    for_each(
        images,
        lambda i: unit(bands + i, pl.multiple_of(rows + i * GROUP, GROUP), GROUP),
    )
    partial[...] = dot_nt(joined[...], w_cat[...])
    send_blocks(place[0], parts, partial, quarter, special)


def stream_back_kernel(sizes, *refs):
    tp_count, quarter = sizes
    parts = refs[:tp_count]
    stream, grad_mid, weight, gain, early = refs[tp_count : tp_count + 5]
    out, send, small = refs[tp_count + 5 :]
    incoming = parts[0][...]
    for k in range(1, tp_count):
        incoming += parts[k][...].astype(f32)
    unit, scaling = norm_parts(stream[...])
    result = grad_mid[...] + norm_back(unit, scaling, incoming * gain[...])
    out[...] = result
    weighted = incoming * weight[...]
    first = jnp.sum(weighted * unit, axis=0, keepdims=True)
    second = jnp.sum(weighted, axis=0, keepdims=True)
    sums = jnp.concatenate([first, second, early[2:8]], axis=0)
    small[...] = sums
    send[:quarter] = result[:quarter].astype(bf16)
    high = sums.astype(bf16)
    send[quarter : quarter + 16] = jnp.concatenate(
        [high.astype(f32), sums - high.astype(f32)], axis=0
    ).astype(bf16)


def join_kernel(sizes, place, *refs):
    tp_count, quarter = sizes
    parts = refs[:tp_count]
    out = refs[tp_count]
    me = place[0]
    for k in range(tp_count):
        spot = lax.rem(me - k + tp_count, tp_count)
        out[pl.ds(pl.multiple_of(spot * quarter, 16), quarter)] = parts[k][:quarter]
        out[pl.ds(pl.multiple_of(quarter * tp_count + spot * 16, 16), 16)] = parts[k][quarter:]


def position_kernel(sizes, slots, images_at, origin, *refs):
    blocks_count, images, rows, tp_count = sizes
    blocks = refs[:blocks_count]
    out, small, ordered, tiny, big, low = refs[blocks_count:]
    per_block = rows // BAND
    slot_count = blocks_count * per_block
    in_band = lax.broadcasted_iota(jnp.int32, (BAND, 1), 0)
    for b in range(blocks_count):
        spot = origin[b]
        tiny[pl.ds(pl.multiple_of(spot * tp_count * 16, 16), tp_count * 16)] = blocks[b][
            rows:
        ].astype(f32)

        def put(j, b=b):
            slot = b * per_block + j
            valid = slots[2 * slot_count + slot]

            @pl.when(valid > 0)
            def _():
                at = pl.multiple_of(slots[3 * slot_count + slot], BAND)
                source = blocks[b][pl.ds(pl.multiple_of(j * BAND, BAND), BAND)]
                ordered[pl.ds(at, BAND)] = jnp.where(in_band < valid, source.astype(f32), 0.0)

        for_each(per_block, put)
    total = tiny[0:16]
    for i in range(1, blocks_count * tp_count):
        total += tiny[i * 16 : (i + 1) * 16]
    small[...] = total[:8] + total[8:]
    big[...] = jnp.zeros_like(big)
    low[...] = jnp.zeros_like(low)

    def add(i):
        at = pl.multiple_of(images_at[i], BAND)
        is_big = images_at[images + i] > 0

        @pl.when(is_big)
        def _():
            big[...] += ordered[pl.ds(at, big.shape[0])]

        @pl.when(jnp.logical_not(is_big))
        def _():
            low[...] += ordered[pl.ds(at, low.shape[0])]

    for_each(images, add)
    out[:PATCH_BIG] = big[:PATCH_BIG]
    out[PATCH_BIG:] = low[: out.shape[0] - PATCH_BIG]


def rotated(x, k):
    count = lax.axis_size("tp")
    return lax.ppermute(x, "tp", [(i, (i + k) % count) for i in range(count)])


def from_group(x):
    return [x] + [rotated(x, k) for k in range(1, lax.axis_size("tp"))]


def to_group(blocks):
    return [blocks[0]] + [rotated(blocks[k], k) for k in range(1, len(blocks))]


def partner(x, k):
    count = lax.axis_size("seq")
    return lax.ppermute(x, "seq", [(i, i ^ k) for i in range(count)])


def from_bands(x):
    if lax.axis_size("seq") != 8:
        return [lax.all_gather(x, "seq", axis=0, tiled=True)]
    even = [x] + [partner(x, k) for k in (2, 4, 6)]
    odd = [partner(block, 1) for block in even]
    return [block for pair in zip(even, odd) for block in pair]


def after(value, *others):
    return lax.optimization_barrier((value,) + tuple(others))[0]


def pad_special(rows, group):
    width = rows.shape[1]
    grouped = rows.reshape(-1, SPECIALS, width)
    return jnp.pad(grouped, ((0, 0), (0, group - SPECIALS), (0, 0))).reshape(-1, width)


def cut_special(rows):
    width = rows.shape[1]
    return rows.reshape(-1, GROUP, width)[:, :SPECIALS].reshape(-1, width)


def joined_columns(query, key, value, axis):
    cut = functools.partial(lax.slice_in_dim, axis=axis)
    return jnp.concatenate(
        [
            query,
            jnp.zeros_like(cut(query, 0, DH)),
            key,
            cut(value, 2 * DH, 3 * DH),
            cut(value, 0, 2 * DH),
        ],
        axis=axis,
    )


def split_columns(joined):
    cut = functools.partial(lax.slice_in_dim, joined, axis=-1)
    return (
        cut(0, 3 * DH),
        cut(4 * DH, 7 * DH),
        jnp.concatenate([cut(8 * DH, 10 * DH), cut(7 * DH, 8 * DH)], axis=-1),
    )


def on_device(
    patches,
    specials,
    pos_table,
    image_length,
    slot_band,
    w_qkv,
    qv_bias,
    w_out,
    branch_bias,
    ln_gain,
    ln_bias,
    layer_scale,
    w_up,
    up_bias,
    w_down,
    cot_patch,
    cot_special,
):
    seq_count = lax.axis_size("seq")
    tp_count = lax.axis_size("tp")
    seq_place = lax.axis_index("seq")
    tp_place = lax.axis_index("tp")
    quarter, width = patches.shape
    images = image_length.shape[0]
    rows = quarter * tp_count
    bands = rows // BAND
    slot_count = slot_band.shape[0]
    special = (specials.shape[0] // SPECIALS) * GROUP
    special_rows = special * tp_count
    total = rows + special_rows
    block = quarter + special
    place = jnp.reshape(tp_place, (1,)).astype(jnp.int32)

    band_counts = (image_length + BAND - 1) // BAND
    band_starts = jnp.cumsum(band_counts) - band_counts
    used = jnp.sum(band_counts)
    passed = (slot_band[:, None] >= band_starts[None, :]).astype(jnp.int32)
    holder = jnp.sum(passed, axis=1) - 1
    picked = holder[:, None] == jnp.arange(images, dtype=jnp.int32)[None, :]
    first_band = jnp.sum(jnp.where(picked, band_starts[None, :], 0), axis=1)
    holder_length = jnp.sum(jnp.where(picked, image_length[None, :], 0), axis=1)
    slot_used = slot_band < used
    slot_valid = jnp.where(
        slot_used, jnp.clip(holder_length - (slot_band - first_band) * BAND, 0, BAND), 0
    )
    slot_at = jnp.where(slot_used, (slot_band + holder + 1) * BAND, 0)
    image_at = (band_starts + jnp.arange(images, dtype=jnp.int32)) * BAND
    slot_window = jnp.sum(jnp.where(picked, image_at[None, :], 0), axis=1)
    table = jnp.stack([slot_at, holder, slot_valid, slot_band * BAND])
    own_table = lax.dynamic_slice_in_dim(
        jnp.concatenate([table, slot_window[None], holder_length[None], first_band[None]]),
        seq_place * bands,
        bands,
        axis=1,
    )
    windows = jnp.concatenate([jnp.where(own_table[2] > 0, own_table[4], 0), image_at]).astype(
        jnp.int32
    )
    if seq_count == 8:
        origin = jnp.bitwise_xor(jnp.arange(8, dtype=jnp.int32), seq_place.astype(jnp.int32))
        slots = table.reshape(4, 8, bands)[:, origin].reshape(-1)
    else:
        origin = jnp.zeros((1,), jnp.int32)
        slots = table.reshape(-1)
    slots = slots.astype(jnp.int32)
    in_band = jnp.arange(BAND, dtype=jnp.int32)
    row_used = in_band[None, :] < own_table[2][:, None]
    row_image = jnp.where(row_used, own_table[1][:, None], -1).reshape(rows, 1)
    group_row = jnp.arange(special_rows, dtype=jnp.int32)
    special_used = group_row % GROUP < SPECIALS
    special_image = jnp.where(special_used, group_row // GROUP, -1)[:, None]
    all_image = jnp.concatenate([row_image, special_image], axis=0)
    first = (seq_place == 0).astype(f32)
    all_weight = jnp.concatenate([jnp.ones((rows,), f32), special_used.astype(f32) * first])[
        :, None
    ]
    own_weight = jnp.concatenate(
        [jnp.ones((quarter,), f32), special_used[:special].astype(f32) * first]
    )[:, None]
    weight_b = all_weight.astype(bf16)

    x_own = jnp.concatenate([patches, pad_special(specials, GROUP)], axis=0)
    x_parts = from_group(x_own)
    offset = jnp.where(own_table[5] == PATCH_BIG, 0, PATCH_BIG)
    position = offset[:, None] + (own_table[0] // BAND - own_table[1] - 1 - own_table[6])[
        :, None
    ] * BAND + in_band[None, :]
    position = jnp.where(row_used, position, 0).reshape(-1)
    pos_rows = jnp.where(row_used.reshape(-1, 1), pos_table[position], 0)
    w_cat = joined_columns(w_qkv[0], w_qkv[1], w_qkv[2], 1)
    b_cat = joined_columns(qv_bias[:1], jnp.zeros_like(qv_bias[:1]), qv_bias[1:], 1)
    w_out_pad = jnp.concatenate(
        [w_out[: 2 * DH], jnp.zeros_like(w_out[:DH]), w_out[2 * DH :]], axis=0
    )
    cot_all = jnp.concatenate([cot_patch, pad_special(cot_special, GROUP)], axis=0)
    grad_two = (cot_all.astype(f32) * layer_scale[1]).astype(bf16)
    grad_hidden = dot_nt(grad_two, w_down)
    grad_result = jnp.concatenate(
        [
            lax.dynamic_slice_in_dim(cot_patch, tp_place * quarter, quarter),
            pad_special(
                lax.dynamic_slice_in_dim(
                    cot_special, tp_place * specials.shape[0], specials.shape[0]
                ),
                GROUP,
            ),
        ],
        axis=0,
    ).astype(f32)

    stream, stream_own, normed, query, pack, key_own, value_own = call(
        functools.partial(embed_kernel, (tp_count, quarter, special, images)),
        [
            ((total, width), f32),
            ((block, width), f32),
            ((total, width), bf16),
            ((total, LANES), bf16),
            ((total, 384), bf16),
            ((total, LANES), bf16),
            ((total, LANES), bf16),
        ],
        [place, *x_parts, pos_rows, w_cat, b_cat, ln_gain[:1], ln_bias[:1], all_image],
    )
    w_outs = from_group(after(w_out_pad, x_parts))

    buffer_rows = (slot_count + images) * BAND + WINDOW
    pairs = from_bands(pack[:rows])
    keys, values, attended, attended_b, query = call(
        functools.partial(attend_kernel, (len(pairs), bands, images, rows)),
        [
            ((buffer_rows, LANES), bf16),
            ((buffer_rows, LANES), bf16),
            ((total, LANES), f32),
            ((total, LANES), bf16),
            ((total, LANES), bf16),
        ],
        [slots, windows, *pairs, key_own, value_own, query],
    )
    attended_all = from_group(attended_b)
    queries = from_bands(query[:rows])

    feed = call(
        functools.partial(feed_kernel, (tp_count, quarter, special)),
        [
            ((block, width), f32),
            ((block, width), f32),
            ((total, width), bf16),
            ((total, w_up.shape[1]), bf16),
            ((total, w_up.shape[1]), bf16),
            ((block, width), f32),
        ]
        + [((block, width), bf16)] * (tp_count - 1),
        [
            place,
            *attended_all,
            *w_outs,
            stream,
            layer_scale,
            branch_bias,
            ln_gain[1:],
            ln_bias[1:],
            w_up,
            up_bias[None],
            grad_hidden,
        ],
        [pltpu.VMEM((total, width), f32), pltpu.VMEM((total, width), f32)],
    )
    mid_own, one_own, normed_two, hidden, grad_pre = feed[:5]
    two_parts = to_group(feed[5:])

    back = call(
        functools.partial(mid_back_kernel, tp_count),
        [((block, width), f32), ((block, width), bf16), ((8, width), f32)]
        + [((block, LANES), bf16)] * tp_count,
        [
            *two_parts,
            mid_own,
            one_own,
            grad_result,
            own_weight,
            layer_scale,
            branch_bias,
            ln_gain[1:],
            *w_outs,
        ],
    )
    grad_mid, grad_one, early = back[:3]
    attn_parts = to_group(back[3:])
    (grad_attn,) = call(
        functools.partial(delta_kernel, (tp_count, quarter, special)),
        [((total, LANES), bf16)],
        [place, *attn_parts, attended],
        [pltpu.VMEM((total, LANES), f32)],
    )
    grads = from_bands(grad_attn[:rows])

    grad_two_w = grad_two * weight_b
    grad_pre_w = grad_pre * weight_b
    down_grad = dot_tn(hidden, grad_two_w)
    up_grad = dot_tn(normed_two, grad_pre_w)
    up_bias_grad = jnp.sum(grad_pre_w.astype(f32), axis=0)
    feed_sums = lax.psum(
        jnp.concatenate(
            [down_grad, up_grad, jnp.pad(up_bias_grad[None], ((0, 15), (0, 0)))], axis=0
        ).astype(bf16),
        "seq",
    ).astype(f32)
    ff = w_up.shape[1]
    down_grad, up_grad, up_bias_grad = (
        feed_sums[:ff],
        feed_sums[ff : ff + width],
        feed_sums[ff + width],
    )
    two_partial = after(dot(hidden, w_down).astype(bf16), attn_parts)
    two_blocks = []
    for k in range(tp_count):
        spot = lax.rem(tp_place + k, tp_count)
        two_blocks.append(
            jnp.concatenate(
                [
                    lax.dynamic_slice_in_dim(two_partial, spot * quarter, quarter),
                    lax.dynamic_slice_in_dim(two_partial, rows + spot * special, special),
                ],
                axis=0,
            )
        )
    branch_two = sum(b.astype(f32) for b in to_group(two_blocks)) + branch_bias[1]
    result = (mid_own + layer_scale[1] * branch_two).astype(bf16)
    weighted_result = grad_result * own_weight
    scale_grad_two = jnp.sum(weighted_result * branch_two, axis=0)
    bias_grad_two = jnp.sum(weighted_result, axis=0) * layer_scale[1]
    early_rows = jnp.concatenate(
        [jnp.zeros((2, width), f32), early[:4], scale_grad_two[None], bias_grad_two[None]], axis=0
    )
    grad_one_all = from_group(after(grad_one, attn_parts))

    (grad_query,) = call(
        functools.partial(query_grad_kernel, (bands, images, rows)),
        [((total, LANES), bf16)],
        [windows, query, grad_attn, keys, values],
    )
    pair = call(
        functools.partial(
            pair_grad_kernel, (len(grads), bands, images, tp_count, quarter, special)
        ),
        [((total, 640), bf16), ((block, width), f32)]
        + [((block, width), bf16)] * (tp_count - 1),
        [
            place,
            slots,
            windows,
            *queries,
            *grads,
            query,
            grad_attn,
            key_own,
            value_own,
            grad_query,
            w_cat,
        ],
        [
            pltpu.VMEM((buffer_rows, LANES), bf16),
            pltpu.VMEM((buffer_rows, LANES), bf16),
            pltpu.VMEM((total, width), f32),
        ],
        outside=(3, 4) if len(grads) == 1 else (),
    )
    joined = pair[0]
    normed_parts = to_group(pair[1:])

    joined_w = joined * weight_b
    qkv_grad = dot_tn(normed, joined_w)
    joined_bias = jnp.sum(joined_w.astype(f32), axis=0)
    out_grad = jnp.zeros((LANES, width), f32)
    for k in range(tp_count):
        spot = lax.rem(tp_place - k + tp_count, tp_count)
        piece = jnp.concatenate(
            [
                lax.dynamic_slice_in_dim(attended_b, spot * quarter, quarter),
                lax.dynamic_slice_in_dim(attended_b, rows + spot * special, special),
            ],
            axis=0,
        )
        out_grad = out_grad + dot_tn(piece, grad_one_all[k] * own_weight.astype(bf16))
    qkv_sums = lax.psum(
        jnp.concatenate([qkv_grad, jnp.pad(joined_bias[None], ((0, 15), (0, 0)))], axis=0).astype(
            bf16
        ),
        "seq",
    ).astype(f32)
    out_sums = lax.psum(out_grad.astype(bf16), "seq").astype(f32)
    out_grad = jnp.concatenate([out_sums[: 2 * DH], out_sums[3 * DH :]], axis=0)
    qkv_grad = jnp.stack(split_columns(qkv_sums[:width]))
    bias_q, _, bias_v = split_columns(qkv_sums[width : width + 1])
    qv_bias_grad = jnp.concatenate([bias_q, bias_v], axis=0)

    grad_stream, send, small = call(
        functools.partial(stream_back_kernel, (tp_count, quarter)),
        [((block, width), f32), ((quarter + 16, width), bf16), ((8, width), f32)],
        [*normed_parts, stream_own, grad_mid, own_weight, ln_gain[:1], early_rows],
    )
    if seq_count == 8:
        (sent,) = call(
            functools.partial(join_kernel, (tp_count, quarter)),
            [((rows + 16 * tp_count, width), bf16)],
            [place, *from_group(send)],
        )
        sent_all = from_bands(sent)
        images_at = jnp.concatenate(
            [band_starts * BAND, (image_length == PATCH_BIG).astype(jnp.int32)]
        ).astype(jnp.int32)
        pos_grad, small = call(
            functools.partial(position_kernel, (len(sent_all), images, rows, tp_count)),
            [((pos_table.shape[0], width), f32), ((8, width), f32)],
            [slots, images_at, origin, *sent_all],
            [
                pltpu.VMEM((slot_count * BAND, width), f32),
                pltpu.VMEM((seq_count * tp_count * 16, width), f32),
                pltpu.VMEM((BIG_BANDS * BAND, width), f32),
                pltpu.VMEM((-(-(pos_table.shape[0] - PATCH_BIG) // BAND) * BAND, width), f32),
            ],
        )
    else:
        mine = lax.dynamic_slice_in_dim(position, tp_place * quarter, quarter)
        used_mine = lax.dynamic_slice_in_dim(row_used.reshape(-1, 1), tp_place * quarter, quarter)
        local = jax.ops.segment_sum(
            jnp.where(used_mine, grad_stream[:quarter], 0.0),
            mine,
            num_segments=pos_table.shape[0],
        )
        pos_grad, small = lax.psum((local, small), ("seq", "tp"))
    return (
        result[:quarter],
        cut_special(result[quarter:]),
        grad_stream[:quarter],
        cut_special(grad_stream[quarter:]),
        pos_grad,
        qkv_grad,
        qv_bias_grad,
        out_grad,
        jnp.stack([small[5], small[7]]),
        jnp.stack([small[0], small[2]]),
        jnp.stack([small[1], small[3]]),
        jnp.stack([small[4], small[6]]),
        up_grad,
        up_bias_grad,
        down_grad,
    )


def solution(mesh):
    in_specs = (
        P(("seq", "tp"), None),
        P("tp", None),
        P(),
        P(),
        P(),
        P(None, None, "tp"),
        P(None, "tp"),
        P("tp", None),
        P(),
        P(),
        P(),
        P(),
        P(None, "tp"),
        P("tp"),
        P("tp", None),
        P("seq", None),
        P(),
    )
    out_specs = (
        P(("seq", "tp"), None),
        P("tp", None),
        P(("seq", "tp"), None),
        P("tp", None),
        P(),
        P(None, None, "tp"),
        P(None, "tp"),
        P("tp", None),
        P(),
        P(),
        P(),
        P(),
        P(None, "tp"),
        P("tp"),
        P("tp", None),
    )
    return jax.shard_map(
        on_device, mesh=mesh, in_specs=in_specs, out_specs=out_specs, check_vma=False
    )
```

time: 655 us -> 403 us (0.62)
  blocking collectives: 226 us -> 0 us
  waiting for transfers between devices: 263 us -> 150 us
  Pallas kernels: 0 us -> 63.6 us
  starting transfers between devices: 8.86 us -> 63.3 us
  matrix products: 63.2 us -> 13 us
  local copies, waits for them, and re-layouts: 45.1 us -> 57.1 us
    psum x2 -> x1, waiting for transfers between devices: 210 us -> 38.4 us  [on_device(): out_sums = lax.psum(out_grad.astype(bf16), 'seq').astype(f32)]
    psum x3 -> x0, blocking collectives: 87.2 us -> none  [the longest x2 45.5 us: on_device(): lax.psum((spec_patch_grads[0], patch_spec_grads[1], patch_spec_grads[2]),...]
    all_gather x6 -> x0, blocking collectives: 76.8 us -> none  [the longest x3 26.2 us: combined_all(): lax.all_gather(a.astype(kind), axis)]
    pallas_call x0 -> x10, Pallas kernels: none -> 63.6 us  [call(): pl.pallas_call(body, out_shape=[jax.ShapeDtypeStruct(s, d) for s, d in ou...]
    unnamed x3 -> x0, blocking collectives: 62.5 us -> none
    ppermute x16 -> x55, starting transfers between devices: 0.93 us -> 63.3 us  [the longest x27 47.9 us: rotated(): return lax.ppermute(x, 'tp', [(i, (i + k) % count) for i in range(count)])]
    ppermute x16 -> x55, waiting for transfers between devices: 52.3 us -> 111 us  [the longest x28 56.2 us: partner(): return lax.ppermute(x, 'seq', [(i, i ^ k) for i in range(count)])]
    dot_general x78 -> x9, matrix products: 62.6 us -> 13 us  [the longest x7 7.55 us: dot_tn(): lax.dot_general(a, b, (((0,), (0,)), ((), ())), preferred_element_type=f32)]
  transfers between devices with their start and end apart: 23 -> 56, of which waited for: 11 -> 21; matrix products, arithmetic and copies ran while one was open for 8% -> 19% of each run, Pallas kernels for 0% -> 14%
where the time goes in v1:
time: 403 us; the launch traced here: 396 us
  waiting for transfers between devices  150 us (37%)
  Pallas kernels  63.6 us (16%)
  starting transfers between devices  63.3 us (16%)
  local copies, waits for them, and re-layouts  57.1 us (14%)
  other arithmetic  34.3 us (9%)
  between operations  15.4 us (4%)
  matrix products  13 us (3%)
    pallas_call x10, Pallas kernels, call(): pl.pallas_call(body, out_shape=[jax.ShapeDtypeStruct(s, d) for s, d in ou...  63.6 us
    ppermute x28, waiting for transfers between devices, partner(): return lax.ppermute(x, 'seq', [(i, i ^ k) for i in range(count)])  56.2 us
    ppermute x27, waiting for transfers between devices, rotated(): return lax.ppermute(x, 'tp', [(i, (i + k) % count) for i in range(count)])  54.9 us
    ppermute x27, starting transfers between devices, rotated(): return lax.ppermute(x, 'tp', [(i, (i + k) % count) for i in range(count)])  47.9 us
    psum x1, waiting for transfers between devices, on_device(): out_sums = lax.psum(out_grad.astype(bf16), 'seq').astype(f32)  38.4 us
    ppermute x28, starting transfers between devices, partner(): return lax.ppermute(x, 'seq', [(i, i ^ k) for i in range(count)])  15.4 us
    unnamed x178, local copies, waits for them, and re-layouts  14.2 us
  transfers between devices with their start and end apart: 56, of which 21 were waited for; matrix products, arithmetic and copies ran while one was open for 19% of the time, Pallas kernels for 14%

profile of v1, /device:TPU:0, one launch (start us, length us, event | category | flops | bytes accessed | tf_op | source)
XLA Modules:
  0.0 396.2 jit_solution(16911570855547920170)
XLA Ops:
  9.7 3.0 collective-permute-start
  12.7 2.6 collective-permute-start.1
  49.4 3.3 fusion.9.refs_15_
  56.0 4.2 %shard_map.280 = (f32[448,768]{1,0:T(8,128)}, f32[112,768]{1,0:T(8,128)}, bf16[448,768]{1,0:T(8,128)(2,1)}, bf16[448,256]{1,0:T(8,128)(2,1)}, bf16[448,384]{1,0:...) custom-call(s32[1]{0:T(128)} %bitcast.place, bf16[112,768]{1,0:T(8,128)(2,1)} %pad_maximum_fusion.3.refs_0_, ...), custom_call_target="tpu_custom_call" | custom-call | tf_op jit(solution)/shard_map/pallas_call | solution.py:104
  64.8 6.4 %collective-permute-done.4.refs_2_ = bf16[384,384]{1,0:T(8,128)(2,1)S(1)} collective-permute-done((bf16[384,384]{1,0:T(8,128)(2,1)S(1)}, bf16[384,384]{1,0:T(8,128)(2,1)S(1)}, u32[]{:S(2)}, u32[]{:S(2)}) %collective-permute-start.4) | collective-permute-done | bytes 294944 | tf_op jit(solution)/shard_map/ppermute | solution.py:557
  72.0 4.7 %collective-permute-done.6.refs_4_ = bf16[384,384]{1,0:T(8,128)(2,1)S(1)} collective-permute-done((bf16[384,384]{1,0:T(8,128)(2,1)S(1)}, bf16[384,384]{1,0:T(8,128)(2,1)S(1)}, u32[]{:S(2)}, u32[]{:S(2)}) %collective-permute-start.6) | collective-permute-done | bytes 294944 | tf_op jit(solution)/shard_map/ppermute | solution.py:557
  78.3 2.6 collective-permute-start.15
  86.1 10.5 %shard_map.281 = (bf16[4864,256]{1,0:T(8,128)(2,1)}, bf16[4864,256]{1,0:T(8,128)(2,1)}, f32[448,256]{1,0:T(8,128)}, bf16[448,256]{1,0:T(8,128)(2,1)}, bf16[448,256]{1,0:T(8,128)(2,1)}) custom-call(s32[192]{0:T(256)} %reshape.358.slots, s32[10]{0:T(128)} %pad_add_fusion.2.windows, bf16[384,384]{1,0:T(8,128)(2,1)} %copy-done.11, bf16[384,384]{1,0:T(8,128)(2,1)} %copy-done.28, ...), custom_call_target="tpu_custom_call" | custom-call | tf_op jit(solution)/shard_map/pallas_call | solution.py:104
  107.3 17.4 %collective-permute-done.11.refs_2_ = bf16[448,256]{1,0:T(8,128)(2,1)S(1)} collective-permute-done((bf16[448,256]{1,0:T(8,128)(2,1)}, bf16[448,256]{1,0:T(8,128)(2,1)S(1)}, u32[]{:S(2)}, u32[]{:S(2)}) %collective-permute-start.11) | collective-permute-done | bytes 229408 | tf_op jit(solution)/shard_map/ppermute | solution.py:544
  125.5 7.3 %shard_map.282 = (f32[112,768]{1,0:T(8,128)}, f32[112,768]{1,0:T(8,128)}, bf16[448,768]{1,0:T(8,128)(2,1)}, bf16[448,768]{1,0:T(8,128)(2,1)}, bf16[448,768]{1,0:...) custom-call(s32[1]{0:T(128)} %bitcast.place, ...), custom_call_target="tpu_custom_call" | custom-call | tf_op jit(solution)/shard_map/pallas_call | solution.py:104
  132.8 5.4 %collective-permute-start.16 = (bf16[112,768]{1,0:T(8,128)(2,1)}, bf16[112,768]{1,0:T(8,128)(2,1)S(1)}, u32[]{:S(2)}, u32[]{:S(2)}) collective-permute-start(bf16[112,768]{1,0:T(8,128)(2,1)} %get-tuple-element.65), channel_id=1, source_target_pairs={{0,1},{1,2},{2,3},{3,0},{4,5},{5,6},{6,7},{7,4},{8,9},{9,10},{10,1... | collective-permute-start | bytes 516104 | tf_op jit(solution)/shard_map/ppermute | solution.py:544
  145.0 4.3 %collective-permute-done.17.refs_2_ = bf16[112,768]{1,0:T(8,128)(2,1)} collective-permute-done((bf16[112,768]{1,0:T(8,128)(2,1)}, bf16[112,768]{1,0:T(8,128)(2,1)}, u32[]{:S(2)}, u32[]{:S(2)}) %collective-permute-start.17) | collective-permute-done | bytes 172064 | tf_op jit(solution)/shard_map/ppermute | solution.py:544
  149.7 3.6 shard_map.283
  153.4 3.9 collective-permute-start.19
  157.3 3.4 collective-permute-start.20
  168.2 2.6 collective-permute-start.23
  177.1 9.4 %shard_map.285.refs_20_ = bf16[448,256]{1,0:T(8,128)(2,1)} custom-call(s32[10]{0:T(128)} %pad_add_fusion.2.windows, bf16[448,256]{1,0:T(8,128)(2,1)} %get-tuple-element.74.query.refs_16_, bf16[448,256]{1,0:T(8,128)(2,1)} %shard_map.284.grad.refs_17_, bf16[4864,256]{1,0:T(8,128)(2,1)} %get-tuple-element.76.keys, bf16[4864,256]{1,0:T(8,128)(2,1)} %get-tuple-element.77.values), custom_call_target="tpu_custom_call" | custom-call | tf_op jit(solution)/shard_map/pallas_call | solution.py:104
  192.1 6.2 %collective-permute-done.52 = bf16[112,768]{1,0:T(8,128)(2,1)S(1)} collective-permute-done((bf16[112,768]{1,0:T(8,128)(2,1)}, bf16[112,768]{1,0:T(8,128)(2,1)S(1)}, u32[]{:S(2)}, u32[]{:S(2)}) %collective-permute-start.52) | collective-permute-done | bytes 172064 | tf_op jit(solution)/shard_map/ppermute | solution.py:544
  201.0 3.4 collective-permute-done.54
  207.5 3.5 collective-permute-done.37.refs_14_
  213.7 13.9 %shard_map.286 = (bf16[448,640]{1,0:T(8,128)(2,1)}, f32[112,768]{1,0:T(8,128)}, bf16[112,768]{1,0:T(8,128)(2,1)}, bf16[112,768]{1,0:T(8,128)(2,1)}, bf16[112,768]{1,0:T(8,128)(2,1)}) custom-call(s32[1]{0:T(128)} %bitcast.place, s32[192]{0:T(256)} %reshape.358.slots, s32[10]{0:T(128)} %pad_add_fusion.2.windows, bf16[384,256]{1,0:T(8,128)(2,1)} %copy-done.12, ...), custom_call_target="tpu_custom_call" | custom-call | tf_op jit(solution)/shard_map/pallas_call | solution.py:104
  233.2 3.9 collective-permute-done.39.refs_1_
  237.1 6.2 %collective-permute-done.40.refs_2_ = bf16[112,768]{1,0:T(8,128)(2,1)S(1)} collective-permute-done((bf16[112,768]{1,0:T(8,128)(2,1)}, bf16[112,768]{1,0:T(8,128)(2,1)S(1)}, u32[]{:S(2)}, u32[]{:S(2)}) %collective-permute-start.40) | collective-permute-done | bytes 172064 | tf_op jit(solution)/shard_map/ppermute | solution.py:544
  244.0 2.6 shard_map.287
  246.6 4.1 %collective-permute-start.42 = (bf16[112,768]{1,0:T(8,128)(2,1)}, bf16[112,768]{1,0:T(8,128)(2,1)S(1)}, u32[]{:S(2)}, u32[]{:S(2)}) collective-permute-start(bf16[112,768]{1,0:T(8,128)(2,1)} %get-tuple-element.86.refs_0_), channel_id=1, source_target_pairs={{0,1},{1,2},{2,3},{3,0},{4,5},{5,6},{6,7},{7,4},{8,9},{9,10},{10,1... | collective-permute-start | bytes 516104 | tf_op jit(solution)/shard_map/ppermute | solution.py:544
  257.2 6.0 %collective-permute-done.43.refs_2_ = bf16[112,768]{1,0:T(8,128)(2,1)S(1)} collective-permute-done((bf16[112,768]{1,0:T(8,128)(2,1)}, bf16[112,768]{1,0:T(8,128)(2,1)S(1)}, u32[]{:S(2)}, u32[]{:S(2)}) %collective-permute-start.43) | collective-permute-done | bytes 172064 | tf_op jit(solution)/shard_map/ppermute | solution.py:544
  274.3 12.7 %collective-permute-done.46.refs_2_ = bf16[448,768]{1,0:T(8,128)(2,1)S(1)} collective-permute-done((bf16[448,768]{1,0:T(8,128)(2,1)}, bf16[448,768]{1,0:T(8,128)(2,1)S(1)}, u32[]{:S(2)}, u32[]{:S(2)}) %collective-permute-start.46) | collective-permute-done | bytes 688160 | tf_op jit(solution)/shard_map/ppermute | solution.py:557
  287.0 3.3 collective-permute-done.48.refs_4_
  290.3 24.4 %collective-permute-done.50.refs_6_ = bf16[448,768]{1,0:T(8,128)(2,1)S(1)} collective-permute-done((bf16[448,768]{1,0:T(8,128)(2,1)}, bf16[448,768]{1,0:T(8,128)(2,1)S(1)}, u32[]{:S(2)}, u32[]{:S(2)}) %collective-permute-start.50) | collective-permute-done | bytes 688160 | tf_op jit(solution)/shard_map/ppermute | solution.py:557
  320.9 7.7 %shard_map.289 = (f32[1625,768]{1,0:T(8,128)}, f32[8,768]{1,0:T(8,128)}) custom-call(s32[192]{0:T(256)} %reshape.358.slots, s32[8]{0:T(128)} %get-tuple-element.218.images_at, s32[8]{0:T(128)} %get-tuple-element.219.origin, bf16[448,768]{1,0:T(8,128)(2,1)} %shard_map.288.refs_0_, bf16[448,768]{1,0:T(8,128)(2,1)} %copy-done.19, bf16[448,768]{1,0:T(8,128)(2,1)} %copy-done.16, ...), custom_call_target="tpu_custom_call" | custom-call | tf_op jit(solution)/shard_map/pallas_call | solution.py:104
  332.2 38.4 %all-reduce.10.cloned.1.call-done = (bf16[256,768]{1,0:T(8,128)(2,1)}, bf16[784,640]{1,0:T(8,128)(2,1)}, bf16[1552,768]{1,0:T(8,128)(2,1)}) async-done(((bf16[256,768]{1,0:T(8,128)(2,1)}, bf16[784,640]{1,0:T(8,128)(2,1)}, bf16[1552,768]{1,0:T(8,128)(2,1)}), (bf16[256,768]{1,0:T(8,128)(2,1)}, bf16[784,640]{1,0:T(8,128)(2,1)}, bf16[1552,768]{1,0:T(8,128)(2,1)})) %all-reduce.10.cloned.1.call-update) | async-done | bytes 3780624 | tf_op jit(solution)/shard_map/psum | solution.py:897
  383.5 2.9 copy.73
  (401 shorter events, 146.7 us)
Async XLA Ops:
  7.2 363.3 %all-reduce.10.cloned.1.call-start = ((), (), s32[]{:S(2)}) async-start(), calls=%async_computation | async-start | bytes 7561216 | tf_op jit(solution)/shard_map/psum | solution.py:897
  9.7 46.3 %collective-permute-start = (bf16[112,768]{1,0:T(8,128)(2,1)}, bf16[112,768]{1,0:T(8,128)(2,1)}, u32[]{:S(2)}, u32[]{:S(2)}) collective-permute-start(bf16[112,768]{1,0:T(8,128)(2,1)} %pad_maximum_fusion.3.refs_0_), channel_id=1, source_target_pairs={{0,1},{1,2},{2,3},{3,0},{4,5},{5,6},{6,7},{7,4},{8,9},{9,10},{10,1... | collective-permute-start | bytes 516104 | tf_op jit(solution)/shard_map/ppermute | solution.py:544
  12.7 43.3 %collective-permute-start.1 = (bf16[112,768]{1,0:T(8,128)(2,1)}, bf16[112,768]{1,0:T(8,128)(2,1)}, u32[]{:S(2)}, u32[]{:S(2)}) collective-permute-start(bf16[112,768]{1,0:T(8,128)(2,1)} %pad_maximum_fusion.3.refs_0_), channel_id=1, source_target_pairs={{0,2},{1,3},{2,0},{3,1},{4,6},{5,7},{6,4},{7,5},{8,10},{9,11},{10,... | collective-permute-start | bytes 516104 | tf_op jit(solution)/shard_map/ppermute | solution.py:544
  15.3 40.7 %collective-permute-start.2 = (bf16[112,768]{1,0:T(8,128)(2,1)}, bf16[112,768]{1,0:T(8,128)(2,1)}, u32[]{:S(2)}, u32[]{:S(2)}) collective-permute-start(bf16[112,768]{1,0:T(8,128)(2,1)} %pad_maximum_fusion.3.refs_0_), channel_id=1, source_target_pairs={{0,3},{1,0},{2,1},{3,2},{4,7},{5,4},{6,5},{7,6},{8,11},{9,8},{10,9... | collective-permute-start | bytes 516104 | tf_op jit(solution)/shard_map/ppermute | solution.py:544
  62.8 13.9 %collective-permute-start.6 = (bf16[384,384]{1,0:T(8,128)(2,1)S(1)}, bf16[384,384]{1,0:T(8,128)(2,1)S(1)}, u32[]{:S(2)}, u32[]{:S(2)}) collective-permute-start(bf16[384,384]{1,0:T(8,128)(2,1)S(1)} %slice.193.refs_0_), channel_id=1, source_target_pairs={{0,16},{4,20},{8,24},{12,28},{16,0},{20,4},{24,8},{28,12},{1,17},{... | collective-permute-start | bytes 884744 | tf_op jit(solution)/shard_map/ppermute | solution.py:557
  64.3 12.4 %collective-permute-start.8 = (bf16[384,384]{1,0:T(8,128)(2,1)S(1)}, bf16[384,384]{1,0:T(8,128)(2,1)S(1)}, u32[]{:S(2)}, u32[]{:S(2)}) collective-permute-start(bf16[384,384]{1,0:T(8,128)(2,1)S(1)} %slice.193.refs_0_), channel_id=1, source_target_pairs={{0,24},{4,28},{8,16},{12,20},{16,8},{20,12},{24,0},{28,4},{1,25},{... | collective-permute-start | bytes 884744 | tf_op jit(solution)/shard_map/ppermute | solution.py:557
  64.8 13.1 %collective-permute-start.3 = (bf16[384,384]{1,0:T(8,128)(2,1)S(1)}, bf16[384,384]{1,0:T(8,128)(2,1)S(1)}, u32[]{:S(2)}, u32[]{:S(2)}) collective-permute-start(bf16[384,384]{1,0:T(8,128)(2,1)S(1)} %slice.193.refs_0_), channel_id=1, source_target_pairs={{0,4},{4,0},{8,12},{12,8},{16,20},{20,16},{24,28},{28,24},{1,5},{5... | collective-permute-start | bytes 884744 | tf_op jit(solution)/shard_map/ppermute | solution.py:557
  71.3 28.2 %collective-permute-start.13 = (bf16[256,768]{1,0:T(8,128)(2,1)S(1)}, bf16[256,768]{1,0:T(8,128)(2,1)S(1)}, u32[]{:S(2)}, u32[]{:S(2)}) collective-permute-start(bf16[256,768]{1,0:T(8,128)(2,1)S(1)} %pad_maximum_fusion.2.refs_4_.refs_11_), channel_id=1, source_target_pairs={{0,1},{1,2},{2,3},{3,0},{4,5},{5,6},{6,7},{7,4},{8,9},{9,10},{10,1... | collective-permute-start | bytes 1179656 | tf_op jit(solution)/shard_map/ppermute | solution.py:544
  77.9 25.2 %collective-permute-start.14 = (bf16[256,768]{1,0:T(8,128)(2,1)S(1)}, bf16[256,768]{1,0:T(8,128)(2,1)S(1)}, u32[]{:S(2)}, u32[]{:S(2)}) collective-permute-start(bf16[256,768]{1,0:T(8,128)(2,1)S(1)} %pad_maximum_fusion.2.refs_4_.refs_11_), channel_id=1, source_target_pairs={{0,2},{1,3},{2,0},{3,1},{4,6},{5,7},{6,4},{7,5},{8,10},{9,11},{10,... | collective-permute-start | bytes 1179656 | tf_op jit(solution)/shard_map/ppermute | solution.py:544
  78.3 25.6 %collective-permute-start.15 = (bf16[256,768]{1,0:T(8,128)(2,1)S(1)}, bf16[256,768]{1,0:T(8,128)(2,1)S(1)}, u32[]{:S(2)}, u32[]{:S(2)}) collective-permute-start(bf16[256,768]{1,0:T(8,128)(2,1)S(1)} %pad_maximum_fusion.2.refs_4_.refs_11_), channel_id=1, source_target_pairs={{0,3},{1,0},{2,1},{3,2},{4,7},{5,4},{6,5},{7,6},{8,11},{9,8},{10,9... | collective-permute-start | bytes 1179656 | tf_op jit(solution)/shard_map/ppermute | solution.py:544
  96.6 28.1 %collective-permute-start.11 = (bf16[448,256]{1,0:T(8,128)(2,1)}, bf16[448,256]{1,0:T(8,128)(2,1)S(1)}, u32[]{:S(2)}, u32[]{:S(2)}) collective-permute-start(bf16[448,256]{1,0:T(8,128)(2,1)} %get-tuple-element.59.refs_0_), channel_id=1, source_target_pairs={{0,2},{1,3},{2,0},{3,1},{4,6},{5,7},{6,4},{7,5},{8,10},{9,11},{10,... | collective-permute-start | bytes 688136 | tf_op jit(solution)/shard_map/ppermute | solution.py:544
  99.5 25.2 %collective-permute-start.12 = (bf16[448,256]{1,0:T(8,128)(2,1)}, bf16[448,256]{1,0:T(8,128)(2,1)S(1)}, u32[]{:S(2)}, u32[]{:S(2)}) collective-permute-start(bf16[448,256]{1,0:T(8,128)(2,1)} %get-tuple-element.59.refs_0_), channel_id=1, source_target_pairs={{0,3},{1,0},{2,1},{3,2},{4,7},{5,4},{6,5},{7,6},{8,11},{9,8},{10,9... | collective-permute-start | bytes 688136 | tf_op jit(solution)/shard_map/ppermute | solution.py:544
  103.1 83.4 %collective-permute-start.26 = (bf16[384,256]{1,0:T(8,128)(2,1)S(1)}, bf16[384,256]{1,0:T(8,128)(2,1)}, u32[]{:S(2)}, u32[]{:S(2)}) collective-permute-start(bf16[384,256]{1,0:T(8,128)(2,1)S(1)} %slice.204.refs_0_), channel_id=1, source_target_pairs={{0,8},{4,12},{8,0},{12,4},{16,24},{20,28},{24,16},{28,20},{1,9},{5... | collective-permute-start | bytes 589832 | tf_op jit(solution)/shard_map/ppermute | solution.py:557
  103.9 85.1 %collective-permute-start.28 = (bf16[384,256]{1,0:T(8,128)(2,1)S(1)}, bf16[384,256]{1,0:T(8,128)(2,1)}, u32[]{:S(2)}, u32[]{:S(2)}) collective-permute-start(bf16[384,256]{1,0:T(8,128)(2,1)S(1)} %slice.204.refs_0_), channel_id=1, source_target_pairs={{0,16},{4,20},{8,24},{12,28},{16,0},{20,4},{24,8},{28,12},{1,17},{... | collective-permute-start | bytes 589832 | tf_op jit(solution)/shard_map/ppermute | solution.py:557
  132.8 12.2 %collective-permute-start.16 = (bf16[112,768]{1,0:T(8,128)(2,1)}, bf16[112,768]{1,0:T(8,128)(2,1)S(1)}, u32[]{:S(2)}, u32[]{:S(2)}) collective-permute-start(bf16[112,768]{1,0:T(8,128)(2,1)} %get-tuple-element.65), channel_id=1, source_target_pairs={{0,1},{1,2},{2,3},{3,0},{4,5},{5,6},{6,7},{7,4},{8,9},{9,10},{10,1... | collective-permute-start | bytes 516104 | tf_op jit(solution)/shard_map/ppermute | solution.py:544
  138.2 11.6 %collective-permute-start.18 = (bf16[112,768]{1,0:T(8,128)(2,1)}, bf16[112,768]{1,0:T(8,128)(2,1)}, u32[]{:S(2)}, u32[]{:S(2)}) collective-permute-start(bf16[112,768]{1,0:T(8,128)(2,1)} %get-tuple-element.67), channel_id=1, source_target_pairs={{0,3},{1,0},{2,1},{3,2},{4,7},{5,4},{6,5},{7,6},{8,11},{9,8},{10,9... | collective-permute-start | bytes 516104 | tf_op jit(solution)/shard_map/ppermute | solution.py:544
  166.7 22.3 %collective-permute-start.22 = (bf16[112,768]{1,0:T(8,128)(2,1)}, bf16[112,768]{1,0:T(8,128)(2,1)S(1)}, u32[]{:S(2)}, u32[]{:S(2)}) collective-permute-start(bf16[112,768]{1,0:T(8,128)(2,1)} %pad_maximum_fusion.4), channel_id=1, source_target_pairs={{0,1},{1,2},{2,3},{3,0},{4,5},{5,6},{6,7},{7,4},{8,9},{9,10},{10,1... | collective-permute-start | bytes 516104 | tf_op jit(solution)/shard_map/ppermute | solution.py:544
  168.2 21.3 %collective-permute-start.23 = (bf16[112,768]{1,0:T(8,128)(2,1)}, bf16[112,768]{1,0:T(8,128)(2,1)S(1)}, u32[]{:S(2)}, u32[]{:S(2)}) collective-permute-start(bf16[112,768]{1,0:T(8,128)(2,1)} %pad_maximum_fusion.5), channel_id=1, source_target_pairs={{0,2},{1,3},{2,0},{3,1},{4,6},{5,7},{6,4},{7,5},{8,10},{9,11},{10,... | collective-permute-start | bytes 516104 | tf_op jit(solution)/shard_map/ppermute | solution.py:544
  171.5 18.1 %collective-permute-start.24 = (bf16[112,768]{1,0:T(8,128)(2,1)}, bf16[112,768]{1,0:T(8,128)(2,1)}, u32[]{:S(2)}, u32[]{:S(2)}) collective-permute-start(bf16[112,768]{1,0:T(8,128)(2,1)} %pad_maximum_fusion.6), channel_id=1, source_target_pairs={{0,3},{1,0},{2,1},{3,2},{4,7},{5,4},{6,5},{7,6},{8,11},{9,8},{10,9... | collective-permute-start | bytes 516104 | tf_op jit(solution)/shard_map/ppermute | solution.py:544
  186.5 13.4 %collective-permute-start.30 = (bf16[384,256]{1,0:T(8,128)(2,1)S(1)}, bf16[384,256]{1,0:T(8,128)(2,1)S(1)}, u32[]{:S(2)}, u32[]{:S(2)}) collective-permute-start(bf16[384,256]{1,0:T(8,128)(2,1)S(1)} %slice.204.refs_0_), channel_id=1, source_target_pairs={{0,24},{4,28},{8,16},{12,20},{16,8},{20,12},{24,0},{28,4},{1,25},{... | collective-permute-start | bytes 589832 | tf_op jit(solution)/shard_map/ppermute | solution.py:557
  189.0 11.5 %collective-permute-start.25 = (bf16[384,256]{1,0:T(8,128)(2,1)S(1)}, bf16[384,256]{1,0:T(8,128)(2,1)S(1)}, u32[]{:S(2)}, u32[]{:S(2)}) collective-permute-start(bf16[384,256]{1,0:T(8,128)(2,1)S(1)} %slice.204.refs_0_), channel_id=1, source_target_pairs={{0,4},{4,0},{8,12},{12,8},{16,20},{20,16},{24,28},{28,24},{1,5},{5... | collective-permute-start | bytes 589832 | tf_op jit(solution)/shard_map/ppermute | solution.py:557
  189.0 16.3 %collective-permute-start.27 = (bf16[384,256]{1,0:T(8,128)(2,1)}, bf16[384,256]{1,0:T(8,128)(2,1)S(1)}, u32[]{:S(2)}, u32[]{:S(2)}) collective-permute-start(bf16[384,256]{1,0:T(8,128)(2,1)} %collective-permute-done.26.refs_2_), channel_id=1, source_target_pairs={{0,4},{4,0},{8,12},{12,8},{16,20},{20,16},{24,28},{28,24},{1,5},{5... | collective-permute-start | bytes 589832 | tf_op jit(solution)/shard_map/ppermute | solution.py:557
  189.5 15.9 %collective-permute-start.29 = (bf16[384,256]{1,0:T(8,128)(2,1)}, bf16[384,256]{1,0:T(8,128)(2,1)S(1)}, u32[]{:S(2)}, u32[]{:S(2)}) collective-permute-start(bf16[384,256]{1,0:T(8,128)(2,1)} %collective-permute-done.28.refs_4_), channel_id=1, source_target_pairs={{0,4},{4,0},{8,12},{12,8},{16,20},{20,16},{24,28},{28,24},{1,5},{5... | collective-permute-start | bytes 589832 | tf_op jit(solution)/shard_map/ppermute | solution.py:557
  211.1 41.9 %collective-permute-start.53 = (bf16[112,768]{1,0:T(8,128)(2,1)}, bf16[112,768]{1,0:T(8,128)(2,1)}, u32[]{:S(2)}, u32[]{:S(2)}) collective-permute-start(bf16[112,768]{1,0:T(8,128)(2,1)} %get-tuple-element.91), channel_id=1, source_target_pairs={{0,2},{1,3},{2,0},{3,1},{4,6},{5,7},{6,4},{7,5},{8,10},{9,11},{10,... | collective-permute-start | bytes 516104 | tf_op jit(solution)/shard_map/ppermute | solution.py:544
  229.5 13.7 %collective-permute-start.40 = (bf16[112,768]{1,0:T(8,128)(2,1)}, bf16[112,768]{1,0:T(8,128)(2,1)S(1)}, u32[]{:S(2)}, u32[]{:S(2)}) collective-permute-start(bf16[112,768]{1,0:T(8,128)(2,1)} %get-tuple-element.80), channel_id=1, source_target_pairs={{0,2},{1,3},{2,0},{3,1},{4,6},{5,7},{6,4},{7,5},{8,10},{9,11},{10,... | collective-permute-start | bytes 516104 | tf_op jit(solution)/shard_map/ppermute | solution.py:544
  250.7 12.5 %collective-permute-start.43 = (bf16[112,768]{1,0:T(8,128)(2,1)}, bf16[112,768]{1,0:T(8,128)(2,1)S(1)}, u32[]{:S(2)}, u32[]{:S(2)}) collective-permute-start(bf16[112,768]{1,0:T(8,128)(2,1)} %get-tuple-element.86.refs_0_), channel_id=1, source_target_pairs={{0,2},{1,3},{2,0},{3,1},{4,6},{5,7},{6,4},{7,5},{8,10},{9,11},{10,... | collective-permute-start | bytes 516104 | tf_op jit(solution)/shard_map/ppermute | solution.py:544
  266.6 20.4 %collective-permute-start.46 = (bf16[448,768]{1,0:T(8,128)(2,1)}, bf16[448,768]{1,0:T(8,128)(2,1)S(1)}, u32[]{:S(2)}, u32[]{:S(2)}) collective-permute-start(bf16[448,768]{1,0:T(8,128)(2,1)} %shard_map.288.refs_0_), channel_id=1, source_target_pairs={{0,8},{4,12},{8,0},{12,4},{16,24},{20,28},{24,16},{28,20},{1,9},{5... | collective-permute-start | bytes 2064392 | tf_op jit(solution)/shard_map/ppermute | solution.py:557
  267.6 22.7 %collective-permute-start.48 = (bf16[448,768]{1,0:T(8,128)(2,1)}, bf16[448,768]{1,0:T(8,128)(2,1)S(1)}, u32[]{:S(2)}, u32[]{:S(2)}) collective-permute-start(bf16[448,768]{1,0:T(8,128)(2,1)} %shard_map.288.refs_0_), channel_id=1, source_target_pairs={{0,16},{4,20},{8,24},{12,28},{16,0},{20,4},{24,8},{28,12},{1,17},{... | collective-permute-start | bytes 2064392 | tf_op jit(solution)/shard_map/ppermute | solution.py:557
  268.1 46.6 %collective-permute-start.50 = (bf16[448,768]{1,0:T(8,128)(2,1)}, bf16[448,768]{1,0:T(8,128)(2,1)S(1)}, u32[]{:S(2)}, u32[]{:S(2)}) collective-permute-start(bf16[448,768]{1,0:T(8,128)(2,1)} %shard_map.288.refs_0_), channel_id=1, source_target_pairs={{0,24},{4,28},{8,16},{12,20},{16,8},{20,12},{24,0},{28,4},{1,25},{... | collective-permute-start | bytes 2064392 | tf_op jit(solution)/shard_map/ppermute | solution.py:557
  274.3 44.8 %collective-permute-start.45 = (bf16[448,768]{1,0:T(8,128)(2,1)S(1)}, bf16[448,768]{1,0:T(8,128)(2,1)S(1)}, u32[]{:S(2)}, u32[]{:S(2)}) collective-permute-start(bf16[448,768]{1,0:T(8,128)(2,1)S(1)} %copy-done.5), channel_id=1, source_target_pairs={{0,4},{4,0},{8,12},{12,8},{16,20},{20,16},{24,28},{28,24},{1,5},{5... | collective-permute-start | bytes 2064392 | tf_op jit(solution)/shard_map/ppermute | solution.py:557
  287.0 32.2 %collective-permute-start.47 = (bf16[448,768]{1,0:T(8,128)(2,1)S(1)}, bf16[448,768]{1,0:T(8,128)(2,1)S(1)}, u32[]{:S(2)}, u32[]{:S(2)}) collective-permute-start(bf16[448,768]{1,0:T(8,128)(2,1)S(1)} %collective-permute-done.46.refs_2_), channel_id=1, source_target_pairs={{0,4},{4,0},{8,12},{12,8},{16,20},{20,16},{24,28},{28,24},{1,5},{5... | collective-permute-start | bytes 2064392 | tf_op jit(solution)/shard_map/ppermute | solution.py:557
  290.3 28.9 %collective-permute-start.49 = (bf16[448,768]{1,0:T(8,128)(2,1)S(1)}, bf16[448,768]{1,0:T(8,128)(2,1)S(1)}, u32[]{:S(2)}, u32[]{:S(2)}) collective-permute-start(bf16[448,768]{1,0:T(8,128)(2,1)S(1)} %collective-permute-done.48.refs_4_), channel_id=1, source_target_pairs={{0,4},{4,0},{8,12},{12,8},{16,20},{20,16},{24,28},{28,24},{1,5},{5... | collective-permute-start | bytes 2064392 | tf_op jit(solution)/shard_map/ppermute | solution.py:557
  (112 other events, 1120.9 us)
Sparse Core Ops, SparseCore 0:
  273.2 97.2 all-reduce.9
